TPU v7x, 32 devices: a whole 2x2x4 slice. The times are simulated.
32 devices in a mesh: wide: 16 (over z, y, x), narrow: 2 (over core).
Axes of the slice: x: 2, y: 2, z: 4, core: 2. Of those that a mesh axis runs over, the one named last changes fastest.
Arguments:
- velocity: bfloat16 [16, 3, 16, 2, 4, 512], P(None, None, 'wide', 'narrow'), may hold values from -160 to 160
- extents: float32 [3, 16, 2, 4], P(None, 'wide', 'narrow'), may hold values from 0.5 to 2
Outputs:
- q_basis: bfloat16 [16, 3, 16, 2, 4, 512], P(None, None, 'wide', 'narrow')
- r_factor: float32 [16, 16], replicated
- dmd_operator: float32 [16, 15], replicated
All inputs are finite; a program needn't handle non-finite values.
Results may differ from a plain program's by a relative error of at most 0.0055.
Values sent between devices are 32-bit elements; how exact they have to be, the bound alone decides.
A program may use at most 128 MiB of HBM per device.

v0:
```python
import math

import jax
import jax.numpy as jnp
import numpy as np
from jax import lax
from jax.sharding import PartitionSpec as P


def padded(cells, sides, width):
    for axis, dim in sides:
        count = lax.axis_size(axis)
        head = lax.slice_in_dim(cells, 0, width, axis=dim)
        tail = lax.slice_in_dim(cells, cells.shape[dim] - width, cells.shape[dim], axis=dim)
        cells = jnp.concatenate(
            [
                lax.ppermute(tail, axis, [(i, (i + 1) % count) for i in range(count)]),
                cells,
                lax.ppermute(head, axis, [((i + 1) % count, i) for i in range(count)]),
            ],
            axis=dim,
        )
    return cells


def gll_tables():
    degree = 7
    node_count = 8
    gll_nodes = np.cos(np.pi * np.arange(node_count) / degree)
    legendre = np.zeros((node_count, node_count))
    for sweep_index in range(60):
        previous = gll_nodes.copy()
        legendre[:, 0] = 1.0
        legendre[:, 1] = previous
        for power in range(2, node_count):
            legendre[:, power] = (
                (2 * power - 1) * previous * legendre[:, power - 1]
                - (power - 1) * legendre[:, power - 2]
            ) / power
        gll_nodes = previous - (previous * legendre[:, degree] - legendre[:, degree - 1]) / (
            node_count * legendre[:, degree]
        )
    legendre[:, 0] = 1.0
    legendre[:, 1] = gll_nodes
    for power in range(2, node_count):
        legendre[:, power] = (
            (2 * power - 1) * gll_nodes * legendre[:, power - 1]
            - (power - 1) * legendre[:, power - 2]
        ) / power
    top_poly = legendre[:, degree][::-1]
    weights = (2.0 / (degree * node_count * legendre[:, degree] ** 2))[::-1]
    ordered = gll_nodes[::-1]
    unit_diag = np.eye(node_count)
    spacing = ordered[:, None] - ordered[None, :] + unit_diag
    derivative = top_poly[:, None] / top_poly[None, :] / spacing
    derivative = derivative * (1.0 - unit_diag)
    derivative[0, 0] = -degree * node_count / 4.0
    derivative[-1, -1] = degree * node_count / 4.0
    return (derivative, weights)


def plane(field, along_axis):
    which = field.ndim + along_axis
    return (
        lax.index_in_dim(field, 0, which, keepdims=False),
        lax.index_in_dim(field, 7, which, keepdims=False),
    )


def add_planes(field, along_axis, from_below, from_above):
    positions = jnp.arange(8)
    plane_shape = [8] + [1] * (-along_axis - 1)
    is_first = (positions == 0).astype(field.dtype).reshape(plane_shape)
    is_last = (positions == 7).astype(field.dtype).reshape(plane_shape)
    return (
        field
        + is_first * jnp.expand_dims(from_below, along_axis)
        + is_last * jnp.expand_dims(from_above, along_axis)
    )


def radial_pass(field):
    low_face, high_face = plane(field, -3)
    zero_plane = jnp.zeros_like(low_face[..., :1, :, :])
    from_below = jnp.concatenate([zero_plane, high_face[..., :-1, :, :]], axis=-3)
    from_above = jnp.concatenate([low_face[..., 1:, :, :], zero_plane], axis=-3)
    return add_planes(field, -3, from_below, from_above)


def face_pair(low_face, high_face, width):
    return jnp.stack([low_face.reshape(-1, width), high_face.reshape(-1, width)], axis=0)


def chol_upper(gram):
    count = gram.shape[0]
    places = jnp.arange(count)
    upper_factor = jnp.zeros((count, count), jnp.float32)
    for column in range(count):
        row_now = gram[column] - jnp.dot(
            upper_factor[:, column], upper_factor, precision=lax.Precision.HIGHEST
        )
        pivot = jnp.sqrt(row_now[column])
        upper_factor = upper_factor.at[column].set(
            jnp.where(places >= column, row_now / pivot, 0.0)
        )
    return upper_factor


def upper_inverse(upper_factor):
    count = upper_factor.shape[0]
    identity_rows = jnp.eye(count, dtype=jnp.float32)
    inverse = jnp.zeros((count, count), jnp.float32)
    for column in range(count - 1, -1, -1):
        row_now = (
            identity_rows[column]
            - jnp.dot(upper_factor[column], inverse, precision=lax.Precision.HIGHEST)
        ) / upper_factor[column, column]
        inverse = inverse.at[column].set(row_now)
    return inverse


def shards(velocity, extents):
    snaps = velocity.shape[0]
    radial = velocity.shape[4]
    width = radial * 64
    derivative, weights = gll_tables()
    rounded = lax.optimization_barrier(jnp.asarray(derivative, jnp.float32).astype(jnp.bfloat16))
    unit_table = rounded.astype(jnp.float32)
    identity_small = jnp.eye(8, dtype=jnp.float32)
    identity_large = jnp.eye(64, dtype=jnp.float32)
    directions = [
        jnp.kron(unit_table, identity_large).T,
        jnp.kron(identity_small, jnp.kron(unit_table, identity_small)).T,
        jnp.kron(identity_large, unit_table).T,
    ]
    norm_weights = jnp.asarray(4.0 * weights, jnp.float32)
    cube_weights = (
        norm_weights[:, None, None] * norm_weights[None, :, None] * norm_weights[None, None, :]
    )
    flow = velocity.reshape(snaps, 3, radial, 512)
    scales = (2.0 / extents).reshape(3, radial)
    halves = []
    for component in range(3):
        table = jnp.concatenate(
            [directions[(component + 1) % 3], directions[(component + 2) % 3]], axis=1
        ).astype(jnp.bfloat16)
        halves.append(
            jnp.einsum("sen,nm->sem", flow[:, component], table, preferred_element_type=jnp.float32)
        )
    vorticity = jnp.stack(
        [
            scales[(component + 1) % 3][:, None] * halves[(component + 2) % 3][..., 512:]
            - scales[(component + 2) % 3][:, None] * halves[(component + 1) % 3][..., :512]
            for component in range(3)
        ],
        axis=1,
    )
    volume = (extents[0] * extents[1] * extents[2]).reshape(radial)
    node_mass = volume[:, None, None, None] * cube_weights
    weighted = radial_pass(node_mass * vorticity.reshape(snaps, 3, radial, 8, 8, 8))
    mass_total = radial_pass(node_mass)
    low_face, high_face = plane(weighted, -1)
    mass_low, mass_high = plane(mass_total, -1)
    received = (
        padded(face_pair(low_face, high_face, width), (("wide", 0),), 1),
        padded(face_pair(mass_low, mass_high, width), (("wide", 0),), 1),
    )
    weighted = add_planes(
        weighted, -1, received[0][0].reshape(low_face.shape), received[0][3].reshape(low_face.shape)
    )
    mass_total = add_planes(
        mass_total,
        -1,
        received[1][0].reshape(mass_low.shape),
        received[1][3].reshape(mass_low.shape),
    )
    low_face, high_face = plane(weighted, -2)
    mass_low, mass_high = plane(mass_total, -2)
    received = (
        padded(face_pair(low_face, high_face, width), (("narrow", 0),), 1),
        padded(face_pair(mass_low, mass_high, width), (("narrow", 0),), 1),
    )
    weighted = add_planes(
        weighted, -2, received[0][0].reshape(low_face.shape), received[0][3].reshape(low_face.shape)
    )
    mass_total = add_planes(
        mass_total,
        -2,
        received[1][0].reshape(mass_low.shape),
        received[1][3].reshape(mass_low.shape),
    )
    rows_local = (jnp.sqrt(node_mass) * (weighted / mass_total)).reshape(snaps, -1)
    local_gram = jnp.dot(rows_local, rows_local.T, precision=lax.Precision.HIGHEST)
    gram_total = lax.psum(local_gram, ("wide", "narrow"))
    upper_factor = chol_upper(gram_total)
    row_count = rows_local.shape[1] * lax.axis_size("wide") * lax.axis_size("narrow")
    inverse = upper_inverse(upper_factor)
    basis = jnp.dot(inverse.T, rows_local, precision=lax.Precision.HIGHEST)
    q_basis = (basis * math.sqrt(row_count)).astype(jnp.bfloat16).reshape(velocity.shape)
    r_factor = upper_factor / math.sqrt(row_count)
    leading_inverse = upper_inverse(upper_factor[: snaps - 1, : snaps - 1])
    dmd_operator = jnp.dot(upper_factor[:, 1:], leading_inverse, precision=lax.Precision.HIGHEST)
    return (q_basis, r_factor, dmd_operator)


def solution(mesh):
    return jax.shard_map(
        shards,
        mesh=mesh,
        in_specs=(P(None, None, "wide", "narrow", None, None), P(None, "wide", "narrow", None)),
        out_specs=(P(None, None, "wide", "narrow", None, None), P(), P()),
        check_vma=False,
    )
```

profile of v0, /device:TPU:0, one launch (start us, length us, event | category | flops | bytes accessed | tf_op | source)
XLA Modules:
  0.0 302.5 jit_solution(3285219728135438394)
XLA Ops:
  4.2 5.4 %multiply_convert_fusion = bf16[64,8,64,8]{3,2,1,0:T(8,128)(2,1)} fusion(f32[8,8]{1,0:T(8,128)S(1)} %convert_element_type.200, f32[64,64]{1,0:T(8,128)S(1)} %fusion.143), kind=kLoop, calls=%fused_computation | loop fusion | flops 524288 | bytes 540928 | tf_op jit(solution)/shard_map/convert.2
  9.7 12.9 %reshape.1455 = bf16[512,512]{1,0:T(8,128)(2,1)S(1)} reshape(bf16[64,8,64,8]{3,2,1,0:T(8,128)(2,1)} %multiply_convert_fusion) | data formatting | bytes 1048576 | tf_op jit(solution)/shard_map/convert.2
  28.1 4.4 %pad_maximum_fusion = (f32[16,3,4,8,8,8]{0,5,4,3,2,1:T(8,128)}, f32[16,3,4,8,8,8]{0,5,4,3,2,1:T(8,128)S(1)}) fusion(f32[16,1,4,8,8,8]{0,5,4,3,2,1:T(8,128)} %bitcast.1001, f32[16,1,4,8,8,8]{0,5,4,3,2,1:T(8,128)} %bitcast.1000, f32[16,1,4,8,8,8]{0,5,4,3,2,1:T(8,128)} %bitcast.999, f32[8,8,8]{2,1,0:T(8,128)S(1)} %broadcast_multiply_fusion.3, ...), kind=kLoop, calls=%fused_computation.3 | loop fusion | flops 296960 | bytes 1181712 | tf_op jit(solution)/shard_map/stack | solution.py:150
  35.6 2.1 copy.45
  37.7 2.1 stack_reshape_squeeze.24
  39.9 2.9 collective-permute-start
  42.8 2.1 copy.47
  44.9 2.1 stack_reshape_squeeze.25
  47.1 4.0 %collective-permute-start.1 = (f32[1,48,256]{2,1,0:T(8,128)}, f32[1,48,256]{2,1,0:T(8,128)}, u32[]{:S(2)}, u32[]{:S(2)}) collective-permute-start(f32[1,48,256]{2,1,0:T(8,128)} %stack_reshape_squeeze.25), channel_id=1, source_target_pairs={{2,0},{4,2},{6,4},{8,6},{10,8},{12,10},{14,12},{16,14},{18,16},{20... | collective-permute-start | bytes 147464 | tf_op jit(solution)/shard_map/ppermute | solution.py:19
  60.5 5.6 %collective-permute-start.5 = (f32[1,1,256]{2,1,0:T(1,128)}, f32[1,1,256]{2,1,0:T(1,128)}, u32[]{:S(2)}, u32[]{:S(2)}) collective-permute-start(f32[1,1,256]{2,1,0:T(1,128)} %stack_reshape_squeeze.29), channel_id=1, source_target_pairs={{2,0},{4,2},{6,4},{8,6},{10,8},{12,10},{14,12},{16,14},{18,16},{20... | collective-permute-start | bytes 3080 | tf_op jit(solution)/shard_map/ppermute | solution.py:19
  67.2 1.8 reduce.137
  71.7 1.8 reduce.136
  84.7 1.8 mul.614
  88.0 1.8 mul.618
  91.2 1.8 mul.623
  94.4 1.8 mul.628
  97.6 1.8 mul.633
  100.9 1.8 mul.638
  105.9 1.8 reduce.139
  110.4 1.8 reduce.138
  114.9 2.1 mul.572
  117.0 2.3 copy.46
  119.3 2.1 mul.576
  121.4 2.3 copy.48
  123.7 2.1 multiply_add_fusion
  136.3 10.9 %fusion.22 = f32[16,16]{1,0:T(8,128)} fusion(f32[16,3,4,8,8,8]{0,5,4,3,2,1:T(8,128)} %copy-done.3, f32[16,3,4,8,8]{0,4,3,2,1:T(8,128)} %copy.52, f32[8]{0:T(128)S(1)} %copy-done.18, f32[16,3,4,8,8]{0,4,3,2,1:T(8,128)} %copy.50, f32[8]{0:T(128)S(1)} %copy-done.21, f32[4,8,8,8]{3,2,0,1:T(8,128)} %copy-done.9, f32[4,8,8,8]{3,2,0,1:T(8,128)} %copy-done.8), kind=kOutput, calls=%fused_computation.40 | convolution fusion | flops 19464192 | bytes 508992 | tf_op jit(solution)/shard_map/dot_general | solution.py:193
  147.2 37.1 %psum.7 = f32[16,16]{1,0:T(8,128)S(1)} all-reduce(f32[16,16]{1,0:T(8,128)} %fusion.22), channel_id=1, replica_groups=mesh['wide'=16,'narrow'=2] {'wide','narrow'}, use_global_device_ids=true, to_apply=%region_0.1 | all-reduce | flops 256 | bytes 2048 | tf_op jit(solution)/shard_map/psum | solution.py:194
  223.3 1.9 fusion.75
  227.2 2.0 fusion.107
  230.5 2.0 fusion.109
  289.6 9.3 %fusion.3 = f32[16,6144]{0,1:T(8,128)S(1)} fusion(f32[16,3,4,8,8,8]{0,5,4,3,2,1:T(8,128)S(1)} %copy-done, f32[6144]{0:T(1024)} %div.376, f32[6144]{0:T(1024)} %mul.643, f32[6144]{0:T(1024)} %mul.638, f32[6144]{0:T(1024)} %mul.633, f32[6144]{0:T(1024)} %mul.628, f32[6144]{0:T(1024)} %mul.623, f32[6144]{0:T(1024)} %mul.618, f32[6144]{0:T(1024)} %mul.614, ...), kind=kLoop, calls=%fused_computation.7 | loop fusion | flops 1474560 | bytes 1302528 | tf_op jit(solution)/shard_map/mul | solution.py:192
  298.9 2.8 fusion
  (296 shorter events, 152.0 us)
Async XLA Ops:
  0.6 3.6 %copy-start.12 = (bf16[16,3,1,1,4,512]{5,4,3,2,1,0:T(4,128)(2,1)S(1)}, bf16[16,3,1,1,4,512]{5,4,3,2,1,0:T(4,128)(2,1)}, u32[]{:S(2)}) copy-start(bf16[16,3,1,1,4,512]{5,4,3,2,1,0:T(4,128)(2,1)} %param.98) | copy-start | bytes 589828
  23.4 4.5 %copy-start.27 = (f32[8]{0:T(128)S(1)}, f32[8]{0:T(128)}, u32[]{:S(2)}) copy-start(f32[8]{0:T(128)} %constant.1149.clone) | copy-start | bytes 100
  23.7 27.3 %copy-start.24 = (f32[4]{0:T(128)}, f32[4]{0:T(128)S(1)}, u32[]{:S(2)}) copy-start(f32[4]{0:T(128)S(1)} %multiply_bitcast_fusion) | copy-start | bytes 52
  23.8 8.9 %copy-start.16 = (f32[8]{0:T(128)}, f32[8]{0:T(128)S(1)}, u32[]{:S(2)}) copy-start(f32[8]{0:T(128)S(1)} %get-tuple-element.613) | copy-start | bytes 100
  23.8 8.9 %copy-start.19 = (f32[8]{0:T(128)}, f32[8]{0:T(128)S(1)}, u32[]{:S(2)}) copy-start(f32[8]{0:T(128)S(1)} %get-tuple-element.614) | copy-start | bytes 100
  28.1 4.4 %copy-start.4 = (f32[8,8,8]{2,1,0:T(8,128)}, f32[8,8,8]{2,1,0:T(8,128)S(1)}, u32[]{:S(2)}) copy-start(f32[8,8,8]{2,1,0:T(8,128)S(1)} %broadcast_multiply_fusion.3) | copy-start | bytes 6148
  39.9 75.0 %collective-permute-start = (f32[1,48,256]{2,1,0:T(8,128)}, f32[1,48,256]{2,1,0:T(8,128)}, u32[]{:S(2)}, u32[]{:S(2)}) collective-permute-start(f32[1,48,256]{2,1,0:T(8,128)} %stack_reshape_squeeze.24), channel_id=1, source_target_pairs={{0,2},{2,4},{4,6},{6,8},{8,10},{10,12},{12,14},{14,16},{16,18},{18... | collective-permute-start | bytes 147464 | tf_op jit(solution)/shard_map/ppermute | solution.py:17
  47.1 72.2 %collective-permute-start.1 = (f32[1,48,256]{2,1,0:T(8,128)}, f32[1,48,256]{2,1,0:T(8,128)}, u32[]{:S(2)}, u32[]{:S(2)}) collective-permute-start(f32[1,48,256]{2,1,0:T(8,128)} %stack_reshape_squeeze.25), channel_id=1, source_target_pairs={{2,0},{4,2},{6,4},{8,6},{10,8},{12,10},{14,12},{16,14},{18,16},{20... | collective-permute-start | bytes 147464 | tf_op jit(solution)/shard_map/ppermute | solution.py:19
  52.5 1.6 copy-start.10
  57.3 9.4 %collective-permute-start.4 = (f32[1,1,256]{2,1,0:T(1,128)}, f32[1,1,256]{2,1,0:T(1,128)}, u32[]{:S(2)}, u32[]{:S(2)}) collective-permute-start(f32[1,1,256]{2,1,0:T(1,128)} %stack_reshape_squeeze.28), channel_id=1, source_target_pairs={{0,2},{2,4},{4,6},{6,8},{8,10},{10,12},{12,14},{14,16},{16,18},{18... | collective-permute-start | bytes 3080 | tf_op jit(solution)/shard_map/ppermute | solution.py:17
  60.5 11.2 %collective-permute-start.5 = (f32[1,1,256]{2,1,0:T(1,128)}, f32[1,1,256]{2,1,0:T(1,128)}, u32[]{:S(2)}, u32[]{:S(2)}) collective-permute-start(f32[1,1,256]{2,1,0:T(1,128)} %stack_reshape_squeeze.29), channel_id=1, source_target_pairs={{2,0},{4,2},{6,4},{8,6},{10,8},{12,10},{14,12},{16,14},{18,16},{20... | collective-permute-start | bytes 3080 | tf_op jit(solution)/shard_map/ppermute | solution.py:19
  75.6 1.6 copy-start.14
  79.2 26.7 %collective-permute-start.6 = (f32[1,1,256]{2,1,0:T(1,128)}, f32[1,1,256]{2,1,0:T(1,128)}, u32[]{:S(2)}, u32[]{:S(2)}) collective-permute-start(f32[1,1,256]{2,1,0:T(1,128)} %stack_reshape_squeeze.30), channel_id=1, source_target_pairs={{0,1},{1,0},{2,3},{3,2},{4,5},{5,4},{6,7},{7,6},{8,9},{9,8},{10,11... | collective-permute-start | bytes 3080 | tf_op jit(solution)/shard_map/ppermute | solution.py:17
  81.9 28.5 %collective-permute-start.7 = (f32[1,1,256]{2,1,0:T(1,128)}, f32[1,1,256]{2,1,0:T(1,128)}, u32[]{:S(2)}, u32[]{:S(2)}) collective-permute-start(f32[1,1,256]{2,1,0:T(1,128)} %stack_reshape_squeeze.31), channel_id=1, source_target_pairs={{1,0},{0,1},{3,2},{2,3},{5,4},{4,5},{7,6},{6,7},{9,8},{8,9},{11,10... | collective-permute-start | bytes 3080 | tf_op jit(solution)/shard_map/ppermute | solution.py:19
  125.8 1.7 copy-start.3
  127.5 2.9 copy-start.5
  127.5 2.9 copy-start.11
  127.5 2.9 copy-start.13
  127.5 2.9 copy-start.15
  127.6 2.9 copy-start.17
  127.6 2.9 copy-start.20
  127.6 2.9 copy-start.22
  127.6 2.9 copy-start.23
  127.6 2.9 copy-start.25
  128.7 4.3 %collective-permute-start.2 = (f32[1,48,256]{2,1,0:T(8,128)S(1)}, f32[1,48,256]{2,1,0:T(8,128)S(1)}, u32[]{:S(2)}, u32[]{:S(2)}) collective-permute-start(f32[1,48,256]{2,1,0:T(8,128)S(1)} %stack_reshape_squeeze.26), channel_id=1, source_target_pairs={{0,1},{1,0},{2,3},{3,2},{4,5},{5,4},{6,7},{7,6},{8,9},{9,8},{10,11... | collective-permute-start | bytes 147464 | tf_op jit(solution)/shard_map/ppermute | solution.py:17
  129.9 4.8 %collective-permute-start.3 = (f32[1,48,256]{2,1,0:T(8,128)S(1)}, f32[1,48,256]{2,1,0:T(8,128)S(1)}, u32[]{:S(2)}, u32[]{:S(2)}) collective-permute-start(f32[1,48,256]{2,1,0:T(8,128)S(1)} %stack_reshape_squeeze.27), channel_id=1, source_target_pairs={{1,0},{0,1},{3,2},{2,3},{5,4},{4,5},{7,6},{6,7},{9,8},{8,9},{11,10... | collective-permute-start | bytes 147464 | tf_op jit(solution)/shard_map/ppermute | solution.py:19
  130.7 2.4 copy-start.8
  131.3 4.9 %copy-start.18 = (f32[8]{0:T(128)S(1)}, f32[8]{0:T(128)}, u32[]{:S(2)}) copy-start(f32[8]{0:T(128)} %copy-done.16) | copy-start | bytes 100
  131.4 4.9 %copy-start.21 = (f32[8]{0:T(128)S(1)}, f32[8]{0:T(128)}, u32[]{:S(2)}) copy-start(f32[8]{0:T(128)} %copy-done.19) | copy-start | bytes 100
  136.3 153.4 %copy-start = (f32[16,3,4,8,8,8]{0,5,4,3,2,1:T(8,128)S(1)}, f32[16,3,4,8,8,8]{0,5,4,3,2,1:T(8,128)}, u32[]{:S(2)}) copy-start(f32[16,3,4,8,8,8]{0,5,4,3,2,1:T(8,128)} %get-tuple-element.576) | copy-start | bytes 1179652
  184.3 3.2 %copy-start.6 = (f32[16,16]{1,0:T(8,128)}, f32[16,16]{1,0:T(8,128)S(1)}, u32[]{:S(2)}) copy-start(f32[16,16]{1,0:T(8,128)S(1)} %psum.7) | copy-start | bytes 3076
  220.6 9.8 %copy-start.1 = (f32[16,16]{1,0:T(8,128)}, f32[16,16]{1,0:T(8,128)S(1)}, u32[]{:S(2)}) copy-start(f32[16,16]{1,0:T(8,128)S(1)} %scatter.184) | copy-start | bytes 3076
  (4 other events, 3.0 us)
where the time goes:
time: 308 us; the launch traced here: 303 us
  local copies, waits for them, and re-layouts  130 us (42%)
  matrix products  74.2 us (24%)
  blocking collectives  37.1 us (12%)
  other arithmetic  35.9 us (12%)
  starting transfers between devices  13.7 us (4%)
  between operations  11.9 us (4%)
    dot_general x31, matrix products, upper_inverse(): jnp.dot(upper_factor[column], inverse, precision=lax.Precision.HIGHEST)  46.4 us
    psum x1, blocking collectives, shards(): gram_total = lax.psum(local_gram, ('wide', 'narrow'))  37.1 us
    mul x14, local copies, waits for them, and re-layouts, add_planes(): is_first * jnp.expand_dims(from_below, along_axis)  21.2 us
    mul x14, local copies, waits for them, and re-layouts, add_planes(): is_last * jnp.expand_dims(from_above, along_axis)  20.4 us
    scatter x31, local copies, waits for them, and re-layouts, upper_inverse(): inverse = inverse.at[column].set(row_now)  19.7 us
    another operation x4, local copies, waits for them, and re-layouts  14.3 us
    dot_general x16, matrix products, chol_upper(): jnp.dot(upper_factor[:, column], upper_factor, precision=lax.Precision.HI...  11.7 us
    dot_general x1, matrix products, shards(): jnp.dot(rows_local, rows_local.T, precision=lax.Precision.HIGHEST)  10.9 us
  transfers between devices with their start and end apart: 8, of which 0 were waited for; matrix products, arithmetic and copies ran while one was open for 23% of the time, Pallas kernels for 0%

commit v1 on v0

v1 whole, which is shorter than its diff:
```python
import functools
import math

import jax
import jax.numpy as jnp
import ml_dtypes
import numpy as np
from jax import lax
from jax.experimental import pallas as pl
from jax.experimental.pallas import tpu as pltpu
from jax.sharding import PartitionSpec as P

MESH = pl.DeviceIdType.MESH
F32 = jnp.float32
BF16 = jnp.bfloat16


def gll_tables():
    degree = 7
    node_count = 8
    gll_nodes = np.cos(np.pi * np.arange(node_count) / degree)
    legendre = np.zeros((node_count, node_count))
    for sweep_index in range(60):
        previous = gll_nodes.copy()
        legendre[:, 0] = 1.0
        legendre[:, 1] = previous
        for power in range(2, node_count):
            legendre[:, power] = (
                (2 * power - 1) * previous * legendre[:, power - 1]
                - (power - 1) * legendre[:, power - 2]
            ) / power
        gll_nodes = previous - (previous * legendre[:, degree] - legendre[:, degree - 1]) / (
            node_count * legendre[:, degree]
        )
    legendre[:, 0] = 1.0
    legendre[:, 1] = gll_nodes
    for power in range(2, node_count):
        legendre[:, power] = (
            (2 * power - 1) * gll_nodes * legendre[:, power - 1]
            - (power - 1) * legendre[:, power - 2]
        ) / power
    top_poly = legendre[:, degree][::-1]
    weights = (2.0 / (degree * node_count * legendre[:, degree] ** 2))[::-1]
    ordered = gll_nodes[::-1]
    unit_diag = np.eye(node_count)
    spacing = ordered[:, None] - ordered[None, :] + unit_diag
    derivative = top_poly[:, None] / top_poly[None, :] / spacing
    derivative = derivative * (1.0 - unit_diag)
    derivative[0, 0] = -degree * node_count / 4.0
    derivative[-1, -1] = degree * node_count / 4.0
    return (derivative, weights)


def tables():
    derivative, weights = gll_tables()
    d8 = derivative.astype(np.float32).astype(ml_dtypes.bfloat16).astype(np.float32)
    i8, i64 = np.eye(8, dtype=np.float32), np.eye(64, dtype=np.float32)
    full = [
        np.kron(d8, i64).T,
        np.kron(i8, np.kron(d8, i8)).T,
        np.kron(i64, d8).T,
    ]
    node = np.arange(512)
    i2, i3 = (node // 8) % 8, node % 8
    picks = np.concatenate([node[i3 == 0], node[i3 == 7], node[i2 == 0], node[i2 == 7]])
    faces = np.concatenate([table[:, picks] for table in full], axis=0)
    spread = np.zeros((2, 128, 512), np.float32)
    for which in range(2):
        spread[which, np.arange(128), picks[128 * which : 128 * which + 128]] = 1.0
    spread = np.concatenate([spread, spread], axis=1)
    cube = weights[:, None, None] * weights[None, :, None] * weights[None, None, :] * 64.0
    root = np.sqrt(cube).reshape(1, 512).astype(np.float32)
    half = lambda table: table.astype(ml_dtypes.bfloat16)
    return (
        half(full[0]),
        half(np.stack([full[1][:256, :256], full[2][:256, :256]])),
        half(faces),
        half(spread),
        root,
    )


def dot(left, right):
    return jnp.dot(left, right, preferred_element_type=F32)


def split(value):
    high = value.astype(BF16)
    low = (value - high.astype(F32)).astype(BF16)
    return high, low


def kernel(
    wide_count,
    narrow_count,
    vel_ref,
    ext_ref,
    first_ref,
    near_ref,
    face_ref,
    spread_ref,
    root_ref,
    q_ref,
    r_ref,
    dmd_ref,
    rows_ref,
    vb_ref,
    send_narrow,
    recv_narrow,
    send_wide,
    recv_wide,
    gram_ref,
    narrow_gram,
    wide_gram,
    face_send_sem,
    face_recv_sem,
    narrow_send_sem,
    narrow_recv_sem,
    wide_send_sem,
    wide_recv_sem,
):
    snaps, _, radial, nodes = vel_ref.shape
    fields = 3 * radial
    blocks = fields + 2 - fields % 2
    pairs = blocks // 2
    row_count = fields * nodes * wide_count * narrow_count
    me_w, me_n = lax.axis_index("wide"), lax.axis_index("narrow")
    wide_at = lambda step: (lax.rem(me_w + step, wide_count), me_n)
    narrow_at = lambda step: (me_w, lax.rem(me_n + step, narrow_count))

    barrier = pltpu.get_barrier_semaphore()
    for step in range(1, narrow_count):
        pl.semaphore_signal(barrier, inc=1, device_id=narrow_at(step), device_id_type=MESH)
    for step in range(1, wide_count):
        pl.semaphore_signal(barrier, inc=1, device_id=wide_at(step), device_id_type=MESH)

    for s in range(snaps):
        for c in range(3):
            value = vel_ref[s, c].astype(F32)
            for j in range(nodes // 128):
                rows_ref[j, pl.ds((s * 3 + c) * radial, radial), :] = value[
                    :, 128 * j : 128 * j + 128
                ]
    for b in range(fields):
        for j in range(nodes // 128):
            vb_ref[pl.ds(b * snaps, snaps), pl.ds(128 * j, 128)] = rows_ref[
                j, pl.ds(b, snaps, stride=fields), :
            ].astype(BF16)
    gram_ref[...] = jnp.zeros_like(gram_ref)
    part = radial * snaps
    comp = lambda c: vb_ref[pl.ds(c * part, part), :]
    pair = [
        jnp.concatenate([comp((k + 1) % 3), comp((k + 2) % 3)], axis=0) for k in range(3)
    ]

    extent = [[ext_ref[k * radial + e] for e in range(radial)] for k in range(3)]
    volume = [extent[0][e] * extent[1][e] * extent[2][e] for e in range(radial)]

    def curl(grads):
        out = []
        for a in range(3):
            b, c = (a + 1) % 3, (a + 2) % 3
            for e in range(radial):
                one = grads[b][e * snaps : (e + 1) * snaps]
                two = grads[c][part + e * snaps : part + (e + 1) * snaps]
                lead = 2.0 * extent[a][e]
                out.append((lead * extent[c][e]) * one - (lead * extent[b][e]) * two)
        return out

    grads = [dot(pair[k], face_ref[pl.ds(k * nodes, nodes), :]) for k in range(3)]
    raw = curl(grads)
    lane = lax.broadcasted_iota(jnp.int32, (snaps, 128), 1)
    place = lane % 64
    at_low, at_high = place < 8, place >= 56
    faces = [[], []]
    for which in range(2):
        cut = [block[:, 128 * which : 128 * which + 128] for block in raw]
        for a in range(3):
            for e in range(radial):
                value = cut[a * radial + e]
                if e > 0:
                    value += jnp.where(at_low, pltpu.roll(cut[a * radial + e - 1], 72, 1), 0.0)
                if e < radial - 1:
                    value += jnp.where(at_high, pltpu.roll(cut[a * radial + e + 1], 56, 1), 0.0)
                faces[which].append(value)
    line = lax.broadcasted_iota(jnp.int32, (snaps, 128), 0)
    mass = jnp.zeros((snaps, 128), F32)
    for e in range(radial):
        row = jnp.full((snaps, 128), volume[e], F32)
        if e > 0:
            row += jnp.where(at_low, volume[e - 1], 0.0)
        if e < radial - 1:
            row += jnp.where(at_high, volume[e + 1], 0.0)
        mass = jnp.where(line == e, row, mass)
    blank = jnp.zeros((snaps, 128), F32)
    for which in range(2):
        faces[which].append(mass)
        while len(faces[which]) < blocks:
            faces[which].append(blank)
    left = lane < 64

    def packed(which, p):
        one, two = faces[which][p], faces[which][p + pairs]
        low = jnp.where(left, one, pltpu.roll(two, 64, 1))
        high = jnp.where(left, pltpu.roll(one, 64, 1), two)
        return low, high

    for p in range(pairs):
        low, high = packed(1, p)
        send_narrow[0, p] = high
        send_narrow[1, p] = low
    wide_faces = [packed(0, p) for p in range(pairs)]

    pl.semaphore_wait(barrier, wide_count + narrow_count - 2)

    def face_copies(source, target, at, count, first):
        return [
            pltpu.make_async_remote_copy(
                src_ref=source.at[way],
                dst_ref=target.at[way],
                send_sem=face_send_sem.at[first + way],
                recv_sem=face_recv_sem.at[first + way],
                device_id=at(1 if way == 0 else count - 1),
                device_id_type=MESH,
            )
            for way in range(2)
        ]

    narrow_copies = face_copies(send_narrow, recv_narrow, narrow_at, narrow_count, 0)
    for copy in narrow_copies:
        copy.start()

    for copy in narrow_copies:
        copy.wait()
    edge_low, edge_high = lane % 8 == 0, lane % 8 == 7
    for p in range(pairs):
        low, high = wide_faces[p]
        below, above = recv_narrow[0, p], recv_narrow[1, p]
        low = low + jnp.where(edge_low, below, 0.0) + jnp.where(
            edge_high, pltpu.roll(above, 7, 1), 0.0
        )
        high = high + jnp.where(edge_high, above, 0.0) + jnp.where(
            edge_low, pltpu.roll(below, 121, 1), 0.0
        )
        send_wide[0, p] = high
        send_wide[1, p] = low
    wide_copies = face_copies(send_wide, recv_wide, wide_at, wide_count, 2)
    for copy in wide_copies:
        copy.start()

    near = [near_ref[0], near_ref[1]]
    whole = [dot(pair[0], first_ref[...])]
    for k in range(2):
        whole.append(
            jnp.concatenate(
                [dot(pair[k + 1][:, :256], near[k]), dot(pair[k + 1][:, 256:], near[k])], axis=1
            )
        )
    raw = curl(whole)
    right = jnp.logical_not(left)
    field = []
    for a in range(3):
        for e in range(radial):
            value = raw[a * radial + e]
            head, tail = value[:, :128], value[:, nodes - 128 :]
            if e > 0:
                last = raw[a * radial + e - 1][:, nodes - 128 :]
                head = head + jnp.where(left, pltpu.roll(last, 64, 1), 0.0)
            if e < radial - 1:
                first = raw[a * radial + e + 1][:, :128]
                tail = tail + jnp.where(right, pltpu.roll(first, 64, 1), 0.0)
            field.append(jnp.concatenate([head, value[:, 128 : nodes - 128], tail], axis=1))
    long_lane = lax.broadcasted_iota(jnp.int32, (snaps, nodes), 1)
    long_line = lax.broadcasted_iota(jnp.int32, (snaps, nodes), 0)
    mass = jnp.ones((snaps, nodes), F32)
    root = jnp.zeros((snaps, nodes), F32)
    for e in range(radial):
        row = jnp.full((snaps, nodes), volume[e], F32)
        size = row
        if e > 0:
            row += jnp.where(long_lane < 64, volume[e - 1], 0.0)
        if e < radial - 1:
            row += jnp.where(long_lane >= nodes - 64, volume[e + 1], 0.0)
        mass = jnp.where(long_line == e, row, mass)
        root = jnp.where(long_line == e, size, root)
    root = jnp.sqrt(root) * root_ref[...]
    field.append(mass)

    def spread(received, which):
        highs, lows = [], []
        for part_of in range(2):
            for p in range(pairs):
                below, above = received[0, p], received[1, p]
                if part_of == 0:
                    both = jnp.where(left, below, pltpu.roll(above, 64, 1))
                else:
                    both = jnp.where(left, pltpu.roll(below, 64, 1), above)
                high, low = split(both)
                highs.append(high)
                lows.append(low)
        stacked = jnp.concatenate(
            [jnp.concatenate(highs, axis=0), jnp.concatenate(lows, axis=0)], axis=1
        )
        return dot(stacked, spread_ref[which])

    extra = spread(recv_narrow, 1)
    field = [value + extra[b * snaps : (b + 1) * snaps] for b, value in enumerate(field)]

    for copy in wide_copies:
        copy.wait()
    extra = spread(recv_wide, 0)
    field = [value + extra[b * snaps : (b + 1) * snaps] for b, value in enumerate(field)]

    scale = root / field[fields]
    highs, lows = [], []
    for b in range(fields):
        e = b % radial
        high, low = split(field[b] * scale[e : e + 1, :])
        highs.append(high)
        lows.append(low)
    high = jnp.concatenate(highs, axis=1)
    low = jnp.concatenate(lows, axis=1)
    both = jnp.concatenate([high, low], axis=0)
    product = lax.dot_general(
        both, both, (((1,), (1,)), ((), ())), preferred_element_type=F32
    )
    gram_ref[:, : 2 * snaps] = product
    product = gram_ref[...]
    top = product[:snaps]
    gram = top + pltpu.roll(top, 128 - snaps, 1) + product[snaps:]
    slim_lane = lax.broadcasted_iota(jnp.int32, (8, 128), 1)
    groups = snaps // 8
    compact = jnp.zeros((8, 128), F32)
    for g in range(groups):
        piece = gram[8 * g : 8 * g + 8]
        if g:
            piece = pltpu.roll(piece, g * snaps, 1)
        inside = jnp.logical_and(slim_lane >= g * snaps, slim_lane < (g + 1) * snaps)
        compact = jnp.where(inside, piece, compact)

    def total(own, buffer, me, at, count, send_sem, recv_sem):
        buffer[me] = own
        copies = [
            pltpu.make_async_remote_copy(
                src_ref=buffer.at[me],
                dst_ref=buffer.at[me],
                send_sem=send_sem.at[step - 1],
                recv_sem=recv_sem.at[step - 1],
                device_id=at(step),
                device_id_type=MESH,
            )
            for step in range(1, count)
        ]
        for copy in copies:
            copy.start()
        for copy in copies:
            copy.wait()
        terms = [buffer[i] for i in range(count)]
        while len(terms) > 1:
            terms = [
                terms[i] + terms[i + 1] if i + 1 < len(terms) else terms[i]
                for i in range(0, len(terms), 2)
            ]
        return terms[0]

    compact = total(
        compact, narrow_gram, me_n, narrow_at, narrow_count, narrow_send_sem, narrow_recv_sem
    )
    compact = total(
        compact, wide_gram, me_w, wide_at, wide_count, wide_send_sem, wide_recv_sem
    )

    lines = [compact]
    for g in range(1, groups):
        lines.append(pltpu.roll(compact, 128 - g * snaps, 1))
    work = jnp.concatenate(lines, axis=0)
    unit = jnp.logical_and(lane % snaps == line, lane < 4 * snaps)
    work = jnp.where(lane < snaps, work, jnp.where(unit, 1.0, 0.0))
    for k in range(snaps - 1):
        lead = work[k : k + 1, :]
        ratio = lead * (1.0 / work[k : k + 1, k : k + 1])
        work = work - jnp.where(line > k, work[:, k : k + 1], 0.0) * ratio
    pivot = jnp.sum(jnp.where(lane == line, work, 0.0), axis=1, keepdims=True)
    work = work * (1.0 / jnp.sqrt(pivot))
    norm = math.sqrt(row_count)
    inverse = pltpu.roll(work, 128 - snaps, 1)
    big, small = split(inverse * norm)
    weights = jnp.where(lane < 2 * snaps, big.astype(F32), small.astype(F32))
    weights = weights[:, : 3 * snaps].astype(BF16)
    basis = dot(weights, jnp.concatenate([both, high], axis=0))
    for b in range(fields):
        q_ref[pl.ds(b * snaps, snaps), :] = basis[:, b * nodes : (b + 1) * nodes].astype(BF16)
    upper = jnp.where(jnp.logical_and(lane >= line, lane < snaps), work, 0.0)
    r_ref[...] = upper[:, :snaps] / norm
    moved = jnp.where(lane < snaps - 1, pltpu.roll(upper, 127, 1), 0.0)
    back = jnp.where(lane < snaps - 1, inverse, 0.0)
    operator = lax.dot_general(
        moved,
        back,
        (((1,), (1,)), ((), ())),
        precision=lax.Precision.HIGHEST,
        preferred_element_type=F32,
    )
    dmd_ref[...] = operator[:, : snaps - 1]


def shards(wide_count, narrow_count, velocity, extents):
    snaps, _, _, _, radial, nodes = velocity.shape
    fields = 3 * radial
    pairs = (fields + 2) // 2
    vmem = pl.BlockSpec(memory_space=pltpu.VMEM)
    face = pltpu.VMEM((2, pairs, snaps, 128), F32)
    dma = pltpu.SemaphoreType.DMA
    q, r, dmd = pl.pallas_call(
        functools.partial(kernel, wide_count, narrow_count),
        out_shape=(
            jax.ShapeDtypeStruct((fields * snaps, nodes), BF16),
            jax.ShapeDtypeStruct((snaps, snaps), F32),
            jax.ShapeDtypeStruct((snaps, snaps - 1), F32),
        ),
        in_specs=[vmem, pl.BlockSpec(memory_space=pltpu.SMEM)] + [vmem] * 5,
        out_specs=(vmem, vmem, vmem),
        scratch_shapes=[
            pltpu.VMEM((nodes // 128, fields * snaps, 128), F32),
            pltpu.VMEM((fields * snaps, nodes), BF16),
            face,
            face,
            face,
            face,
            pltpu.VMEM((2 * snaps, 128), F32),
            pltpu.VMEM((narrow_count, 8, 128), F32),
            pltpu.VMEM((wide_count, 8, 128), F32),
            dma((4,)),
            dma((4,)),
            dma((narrow_count - 1,)),
            dma((narrow_count - 1,)),
            dma((wide_count - 1,)),
            dma((wide_count - 1,)),
        ],
        compiler_params=pltpu.CompilerParams(
            collective_id=0, has_side_effects=True, vmem_limit_bytes=32 * 1024 * 1024
        ),
        cost_estimate=pl.CostEstimate(
            flops=400_000_000, bytes_accessed=3_000_000, transcendentals=10_000
        ),
        name="pipe",
    )(
        velocity.reshape(snaps, 3, radial, nodes),
        extents.reshape(3 * radial),
        *[jnp.asarray(table) for table in tables()],
    )
    q = jnp.transpose(q.reshape(3, radial, snaps, nodes), (2, 0, 1, 3))
    return q.reshape(velocity.shape), r, dmd


def solution(mesh):
    return jax.shard_map(
        functools.partial(shards, mesh.shape["wide"], mesh.shape["narrow"]),
        mesh=mesh,
        in_specs=(P(None, None, "wide", "narrow", None, None), P(None, "wide", "narrow", None)),
        out_specs=(P(None, None, "wide", "narrow", None, None), P(), P()),
        check_vma=False,
    )
```

time: 308 us -> 31.4 us (0.10); the launches traced: 303 us -> 31 us
  local copies, waits for them, and re-layouts: 130 us -> 8.47 us
  matrix products: 74.2 us -> 0 us
  blocking collectives: 37.1 us -> 0 us
  other arithmetic: 35.9 us -> 0.02 us
  Pallas kernels: 0 us -> 21.9 us
  starting transfers between devices: 13.7 us -> 0 us
  between operations: 11.9 us -> 0.66 us
    dot_general x53 -> x0, matrix products: 74.2 us -> none  [the longest x31 46.4 us: upper_inverse(): jnp.dot(upper_factor[column], inverse, precision=lax.Precision.HIGHEST)]
    mul x35 -> x0, local copies, waits for them, and re-layouts: 46 us -> none  [the longest x14 21.2 us: add_planes(): is_first * jnp.expand_dims(from_below, along_axis)]
    psum x1 -> x0, blocking collectives: 37.1 us -> none  [shards(): gram_total = lax.psum(local_gram, ('wide', 'narrow'))]
    slice x47 -> x0, local copies, waits for them, and re-layouts: 27 us -> none  [the longest x15 8.91 us: chol_upper(): pivot = jnp.sqrt(row_now[column])]
    another operation x12 -> x0, local copies, waits for them, and re-layouts: 24.8 us -> none
    pallas_call x0 -> x1, Pallas kernels: none -> 21.9 us  [shards(): pl.pallas_call(functools.partial(kernel, wide_count, narrow_count), out_s...]
    scatter x47 -> x0, local copies, waits for them, and re-layouts: 20.9 us -> none  [the longest x31 19.7 us: upper_inverse(): inverse = inverse.at[column].set(row_now)]
    ppermute x8 -> x0, starting transfers between devices: 13.7 us -> none  [the longest x4 10.7 us: padded(): lax.ppermute(head, axis, [((i + 1) % count, i) for i in range(count)])]
  transfers between devices with their start and end apart: 8 -> 0, of which waited for: 0 -> 0; matrix products, arithmetic and copies ran while one was open for 23% -> 0% of each run, Pallas kernels for 0% -> 0%
where the time goes in v1:
time: 31.4 us; the launch traced here: 31 us
  Pallas kernels  21.9 us (70%)
  local copies, waits for them, and re-layouts  8.47 us (27%)
  between operations  0.66 us (2%)
    pallas_call x1, Pallas kernels, shards(): pl.pallas_call(functools.partial(kernel, wide_count, narrow_count), out_s...  21.9 us
    unnamed x16, local copies, waits for them, and re-layouts  7.56 us
    reshape x1, local copies, waits for them, and re-layouts, shards(): q = jnp.transpose(q.reshape(3, radial, snaps, nodes), (2, 0, 1, 3))  0.83 us

profile of v1, /device:TPU:0, one launch (start us, length us, event | category | flops | bytes accessed | tf_op | source)
XLA Modules:
  0.0 31.0 jit_solution(1804105276826977303)
XLA Ops:
  0.6 0.0 copy-start.6
  0.6 0.7 %copy-done.6 = f32[3,1,1,4]{3,2,1,0:T(1,128)S(1)} copy-done((f32[3,1,1,4]{3,2,1,0:T(1,128)S(1)}, f32[3,1,1,4]{3,2,1,0:T(1,128)}, u32[]{:S(2)}) %copy-start.6) | copy-done | bytes 72
  1.3 0.0 copy-start.5
  1.3 0.1 reshape.19.ext_ref
  1.4 0.6 %copy-done.5 = f32[1,512]{1,0:T(1,128)S(1)} copy-done((f32[1,512]{1,0:T(1,128)S(1)}, f32[1,512]{1,0:T(1,128)}, u32[]{:S(2)}) %copy-start.5) | copy-done | bytes 2072
  2.0 0.0 copy-start
  2.0 1.1 %copy-done = bf16[1536,256]{1,0:T(8,128)(2,1)S(1)} copy-done((bf16[1536,256]{1,0:T(8,128)(2,1)S(1)}, bf16[1536,256]{1,0:T(8,128)(2,1)}, u32[]{:S(2)}) %copy-start) | copy-done | bytes 786456
  3.1 0.0 copy-start.1
  3.1 1.0 %copy-done.1 = bf16[2,256,512]{2,1,0:T(8,128)(2,1)S(1)} copy-done((bf16[2,256,512]{2,1,0:T(8,128)(2,1)S(1)}, bf16[2,256,512]{2,1,0:T(8,128)(2,1)}, u32[]{:S(2)}) %copy-start.1) | copy-done | bytes 524312
  4.2 0.0 copy-start.2
  4.2 1.0 %copy-done.2 = bf16[512,512]{1,0:T(8,128)(2,1)S(1)} copy-done((bf16[512,512]{1,0:T(8,128)(2,1)S(1)}, bf16[512,512]{1,0:T(8,128)(2,1)}, u32[]{:S(2)}) %copy-start.2) | copy-done | bytes 524312
  5.2 0.0 copy-start.3
  5.2 0.9 %copy-done.3 = bf16[2,256,256]{2,1,0:T(8,128)(2,1)S(1)} copy-done((bf16[2,256,256]{2,1,0:T(8,128)(2,1)S(1)}, bf16[2,256,256]{2,1,0:T(8,128)(2,1)}, u32[]{:S(2)}) %copy-start.3) | copy-done | bytes 262168
  6.2 0.0 copy-start.4
  6.2 0.9 %copy-done.4 = bf16[16,3,1,1,4,512]{5,4,3,2,1,0:T(4,128)(2,1)S(1)} copy-done((bf16[16,3,1,1,4,512]{5,4,3,2,1,0:T(4,128)(2,1)S(1)}, bf16[16,3,1,1,4,512]{5,4,3,2,1,0:T(4,128)(2,1)}, u32[]{:S(2)}) %copy-start.4) | copy-done | bytes 196632
  7.1 21.9 %pipe.1 = (bf16[192,512]{1,0:T(8,128)(2,1)S(1)}, f32[16,16]{1,0:T(8,128)S(1)}, f32[16,15]{1,0:T(8,128)S(1)}) custom-call(bf16[16,3,4,512]{3,2,1,0:T(4,128)(2,1)S(1)} %bitcast.7, f32[12]{0:T(128)S(1)} %reshape.19.ext_ref, bf16[512,512]{1,0:T(8,128)(2,1)S(1)} %copy-done.2, bf16[2,256,256]{2,1,0:T(8,128)(2,1)S(1)} %copy-done.3, bf16[1536,256]{1,0:T(8,128)(2,1)S(1)} %copy-done, ...), custom_call_target="tpu_custom_call" | custom-call | flops 400000000 | bytes 3000000 | tf_op jit(solution)/shard_map/pipe/pallas_call | solution.py:414
  29.0 0.8 %copy.12 = bf16[3,4,16,512]{3,1,0,2:T(4,128)(2,1)} copy(bf16[3,4,16,512]{3,2,1,0:T(8,128)(2,1)S(1)} %bitcast.8) | data formatting | bytes 393216 | tf_op jit(solution)/shard_map/reshape | solution.py:452
  29.8 0.6 %copy.15 = f32[16,16]{1,0:T(8,128)} copy(f32[16,16]{1,0:T(8,128)S(1)} %get-tuple-element.13) | data formatting | bytes 2048
  30.4 0.6 %copy.16 = f32[16,15]{1,0:T(8,128)} copy(f32[16,15]{1,0:T(8,128)S(1)} %get-tuple-element.14) | data formatting | bytes 1920
  (1 shorter events, 0.0 us)
Async XLA Ops:
  0.6 0.7 %copy-start.6 = (f32[3,1,1,4]{3,2,1,0:T(1,128)S(1)}, f32[3,1,1,4]{3,2,1,0:T(1,128)}, u32[]{:S(2)}) copy-start(f32[3,1,1,4]{3,2,1,0:T(1,128)} %param.8) | copy-start | bytes 148
  1.3 0.7 %copy-start.5 = (f32[1,512]{1,0:T(1,128)S(1)}, f32[1,512]{1,0:T(1,128)}, u32[]{:S(2)}) copy-start(f32[1,512]{1,0:T(1,128)} %constant.14.clone.root_ref) | copy-start | bytes 6148
  2.0 1.1 %copy-start = (bf16[1536,256]{1,0:T(8,128)(2,1)S(1)}, bf16[1536,256]{1,0:T(8,128)(2,1)}, u32[]{:S(2)}) copy-start(bf16[1536,256]{1,0:T(8,128)(2,1)} %constant.12.clone.face_ref) | copy-start | bytes 2359300
  3.1 1.0 %copy-start.1 = (bf16[2,256,512]{2,1,0:T(8,128)(2,1)S(1)}, bf16[2,256,512]{2,1,0:T(8,128)(2,1)}, u32[]{:S(2)}) copy-start(bf16[2,256,512]{2,1,0:T(8,128)(2,1)} %constant.13.clone.spread_ref) | copy-start | bytes 1572868
  4.2 1.0 %copy-start.2 = (bf16[512,512]{1,0:T(8,128)(2,1)S(1)}, bf16[512,512]{1,0:T(8,128)(2,1)}, u32[]{:S(2)}) copy-start(bf16[512,512]{1,0:T(8,128)(2,1)} %constant.10.clone.first_ref) | copy-start | bytes 1572868
  5.2 0.9 %copy-start.3 = (bf16[2,256,256]{2,1,0:T(8,128)(2,1)S(1)}, bf16[2,256,256]{2,1,0:T(8,128)(2,1)}, u32[]{:S(2)}) copy-start(bf16[2,256,256]{2,1,0:T(8,128)(2,1)} %constant.11.clone.near_ref) | copy-start | bytes 786436
  6.2 0.9 %copy-start.4 = (bf16[16,3,1,1,4,512]{5,4,3,2,1,0:T(4,128)(2,1)S(1)}, bf16[16,3,1,1,4,512]{5,4,3,2,1,0:T(4,128)(2,1)}, u32[]{:S(2)}) copy-start(bf16[16,3,1,1,4,512]{5,4,3,2,1,0:T(4,128)(2,1)} %param.7) | copy-start | bytes 589828

commit v2 on v1

--- a/solution.py
+++ b/solution.py
@@ -93,6 +93,16 @@
 def kernel(
     wide_count,
     narrow_count,
+    vel_in,
+    ext_in,
+    first_in,
+    near_in,
+    face_in,
+    spread_in,
+    root_in,
+    q_ref,
+    r_ref,
+    dmd_ref,
     vel_ref,
     ext_ref,
     first_ref,
@@ -100,20 +110,22 @@
     face_ref,
     spread_ref,
     root_ref,
-    q_ref,
-    r_ref,
-    dmd_ref,
+    load_sem,
     rows_ref,
     vb_ref,
     send_narrow,
     recv_narrow,
     send_wide,
     recv_wide,
+    send_edge,
+    recv_edge,
     gram_ref,
     narrow_gram,
     wide_gram,
     face_send_sem,
     face_recv_sem,
+    edge_send_sem,
+    edge_recv_sem,
     narrow_send_sem,
     narrow_recv_sem,
     wide_send_sem,
@@ -128,12 +140,40 @@
     wide_at = lambda step: (lax.rem(me_w + step, wide_count), me_n)
     narrow_at = lambda step: (me_w, lax.rem(me_n + step, narrow_count))
 
+    loads = [
+        pltpu.make_async_copy(source, target, load_sem.at[i])
+        for i, (source, target) in enumerate(
+            [
+                (vel_in, vel_ref),
+                (ext_in, ext_ref),
+                (face_in, face_ref),
+                (first_in, first_ref),
+                (near_in, near_ref),
+                (spread_in, spread_ref),
+                (root_in, root_ref),
+            ]
+        )
+    ]
+    for load in loads:
+        load.start()
+
     barrier = pltpu.get_barrier_semaphore()
     for step in range(1, narrow_count):
         pl.semaphore_signal(barrier, inc=1, device_id=narrow_at(step), device_id_type=MESH)
     for step in range(1, wide_count):
         pl.semaphore_signal(barrier, inc=1, device_id=wide_at(step), device_id_type=MESH)
-
+    turns = sorted({1, narrow_count - 1})
+    corner_at = lambda step, turn: (
+        lax.rem(me_w + step, wide_count),
+        lax.rem(me_n + turn, narrow_count),
+    )
+    ways = (1, wide_count - 1)
+    for step in ways:
+        for turn in turns:
+            pl.semaphore_signal(
+                barrier, inc=1, device_id=corner_at(step, turn), device_id_type=MESH
+            )
+    loads[0].wait()
     for s in range(snaps):
         for c in range(3):
             value = vel_ref[s, c].astype(F32)
@@ -153,6 +193,7 @@
         jnp.concatenate([comp((k + 1) % 3), comp((k + 2) % 3)], axis=0) for k in range(3)
     ]
 
+    loads[1].wait()
     extent = [[ext_ref[k * radial + e] for e in range(radial)] for k in range(3)]
     volume = [extent[0][e] * extent[1][e] * extent[2][e] for e in range(radial)]
 
@@ -167,6 +208,7 @@
                 out.append((lead * extent[c][e]) * one - (lead * extent[b][e]) * two)
         return out
 
+    loads[2].wait()
     grads = [dot(pair[k], face_ref[pl.ds(k * nodes, nodes), :]) for k in range(3)]
     raw = curl(grads)
     lane = lax.broadcasted_iota(jnp.int32, (snaps, 128), 1)
@@ -209,9 +251,28 @@
         low, high = packed(1, p)
         send_narrow[0, p] = high
         send_narrow[1, p] = low
-    wide_faces = [packed(0, p) for p in range(pairs)]
-
-    pl.semaphore_wait(barrier, wide_count + narrow_count - 2)
+    groups_of = -(-pairs // 4)
+    residue = lane % 8
+    edge_of = [
+        jnp.logical_or(residue == 2 * r, residue == (2 * r + 7) % 8) for r in range(4)
+    ]
+    for g in range(groups_of):
+        edges = [blank, blank]
+        for r in range(4):
+            p = 4 * g + r
+            if p >= pairs:
+                continue
+            low, high = packed(0, p)
+            send_wide[0, p] = high
+            send_wide[1, p] = low
+            for way, value in enumerate((high, low)):
+                if r:
+                    value = pltpu.roll(value, 2 * r, 1)
+                edges[way] = jnp.where(edge_of[r], value, edges[way])
+        for way in range(2):
+            send_edge[way, g] = edges[way]
+
+    pl.semaphore_wait(barrier, wide_count + narrow_count - 2 + 2 * len(turns))
 
     def face_copies(source, target, at, count, first):
         return [
@@ -226,28 +287,25 @@
             for way in range(2)
         ]
 
+    wide_copies = face_copies(send_wide, recv_wide, wide_at, wide_count, 2)
+    edge_copies = [
+        pltpu.make_async_remote_copy(
+            src_ref=send_edge.at[way],
+            dst_ref=recv_edge.at[way, i],
+            send_sem=edge_send_sem.at[way, i],
+            recv_sem=edge_recv_sem.at[way, i],
+            device_id=corner_at(ways[way], turn),
+            device_id_type=MESH,
+        )
+        for way in range(2)
+        for i, turn in enumerate(turns)
+    ]
     narrow_copies = face_copies(send_narrow, recv_narrow, narrow_at, narrow_count, 0)
-    for copy in narrow_copies:
+    for copy in wide_copies + edge_copies + narrow_copies:
         copy.start()
 
-    for copy in narrow_copies:
-        copy.wait()
-    edge_low, edge_high = lane % 8 == 0, lane % 8 == 7
-    for p in range(pairs):
-        low, high = wide_faces[p]
-        below, above = recv_narrow[0, p], recv_narrow[1, p]
-        low = low + jnp.where(edge_low, below, 0.0) + jnp.where(
-            edge_high, pltpu.roll(above, 7, 1), 0.0
-        )
-        high = high + jnp.where(edge_high, above, 0.0) + jnp.where(
-            edge_low, pltpu.roll(below, 121, 1), 0.0
-        )
-        send_wide[0, p] = high
-        send_wide[1, p] = low
-    wide_copies = face_copies(send_wide, recv_wide, wide_at, wide_count, 2)
-    for copy in wide_copies:
-        copy.start()
-
+    for load in loads[3:]:
+        load.wait()
     near = [near_ref[0], near_ref[1]]
     whole = [dot(pair[0], first_ref[...])]
     for k in range(2):
@@ -286,11 +344,21 @@
     root = jnp.sqrt(root) * root_ref[...]
     field.append(mass)
 
+    edge_low, edge_high = residue == 0, residue == 7
+
+    def with_edges(way, p):
+        g, r = p // 4, p % 4
+        pieces = []
+        for slot, places, shift in ((0, edge_low, 121), (len(turns) - 1, edge_high, 7)):
+            piece = pltpu.roll(recv_edge[way, slot, g], (shift - 2 * r) % 128, 1)
+            pieces.append(jnp.where(places, piece, 0.0))
+        return recv_wide[way, p] + (pieces[0] + pieces[1])
+
     def spread(received, which):
         highs, lows = [], []
         for part_of in range(2):
             for p in range(pairs):
-                below, above = received[0, p], received[1, p]
+                below, above = received(0, p), received(1, p)
                 if part_of == 0:
                     both = jnp.where(left, below, pltpu.roll(above, 64, 1))
                 else:
@@ -303,12 +371,14 @@
         )
         return dot(stacked, spread_ref[which])
 
-    extra = spread(recv_narrow, 1)
+    for copy in narrow_copies:
+        copy.wait()
+    extra = spread(lambda way, p: recv_narrow[way, p], 1)
     field = [value + extra[b * snaps : (b + 1) * snaps] for b, value in enumerate(field)]
 
-    for copy in wide_copies:
+    for copy in edge_copies + wide_copies:
         copy.wait()
-    extra = spread(recv_wide, 0)
+    extra = spread(with_edges, 0)
     field = [value + extra[b * snaps : (b + 1) * snaps] for b, value in enumerate(field)]
 
     scale = root / field[fields]
@@ -409,6 +479,13 @@
     fields = 3 * radial
     pairs = (fields + 2) // 2
     vmem = pl.BlockSpec(memory_space=pltpu.VMEM)
+    operands = [
+        velocity.reshape(snaps, 3, radial, nodes),
+        extents.reshape(3 * radial),
+        *[jnp.asarray(table) for table in tables()],
+    ]
+    corners = len({1, narrow_count - 1})
+    edge = (-(-pairs // 4), snaps, 128)
     face = pltpu.VMEM((2, pairs, snaps, 128), F32)
     dma = pltpu.SemaphoreType.DMA
     q, r, dmd = pl.pallas_call(
@@ -418,37 +495,42 @@
             jax.ShapeDtypeStruct((snaps, snaps), F32),
             jax.ShapeDtypeStruct((snaps, snaps - 1), F32),
         ),
-        in_specs=[vmem, pl.BlockSpec(memory_space=pltpu.SMEM)] + [vmem] * 5,
+        in_specs=[pl.BlockSpec(memory_space=pltpu.HBM)] * len(operands),
         out_specs=(vmem, vmem, vmem),
         scratch_shapes=[
+            (pltpu.SMEM if i == 1 else pltpu.VMEM)(operand.shape, operand.dtype)
+            for i, operand in enumerate(operands)
+        ]
+        + [
+            dma((len(operands),)),
             pltpu.VMEM((nodes // 128, fields * snaps, 128), F32),
             pltpu.VMEM((fields * snaps, nodes), BF16),
             face,
             face,
             face,
             face,
+            pltpu.VMEM((2,) + edge, F32),
+            pltpu.VMEM((2, corners) + edge, F32),
             pltpu.VMEM((2 * snaps, 128), F32),
             pltpu.VMEM((narrow_count, 8, 128), F32),
             pltpu.VMEM((wide_count, 8, 128), F32),
             dma((4,)),
             dma((4,)),
+            dma((2, corners)),
+            dma((2, corners)),
             dma((narrow_count - 1,)),
             dma((narrow_count - 1,)),
             dma((wide_count - 1,)),
             dma((wide_count - 1,)),
         ],
         compiler_params=pltpu.CompilerParams(
-            collective_id=0, has_side_effects=True, vmem_limit_bytes=32 * 1024 * 1024
+            collective_id=0, has_side_effects=True, vmem_limit_bytes=60 * 1024 * 1024
         ),
         cost_estimate=pl.CostEstimate(
             flops=400_000_000, bytes_accessed=3_000_000, transcendentals=10_000
         ),
         name="pipe",
-    )(
-        velocity.reshape(snaps, 3, radial, nodes),
-        extents.reshape(3 * radial),
-        *[jnp.asarray(table) for table in tables()],
-    )
+    )(*operands)
     q = jnp.transpose(q.reshape(3, radial, snaps, nodes), (2, 0, 1, 3))
     return q.reshape(velocity.shape), r, dmd
 

time: 31.4 us -> 26.3 us (0.84)
  local copies, waits for them, and re-layouts: 8.47 us -> 4.34 us
  Pallas kernels: 21.9 us -> 21.1 us
    unnamed x16 -> x8, local copies, waits for them, and re-layouts: 7.56 us -> 1.98 us
    reshape x1, local copies, waits for them, and re-layouts: 0.83 us -> 1.76 us  [shards(): q = jnp.transpose(q.reshape(3, radial, snaps, nodes), (2, 0, 1, 3))]
    pallas_call x1, Pallas kernels: 21.9 us -> 21.1 us  [shards(): pl.pallas_call(functools.partial(kernel, wide_count, narrow_count), out_s...]
    reshape x1, local copies, waits for them, and re-layouts: 0.08 us -> 0.6 us  [shards(): extents.reshape(3 * radial)]
where the time goes in v2:
time: 26.3 us; the launch traced here: 26.1 us
  Pallas kernels  21.1 us (80%)
  local copies, waits for them, and re-layouts  4.34 us (17%)
  between operations  0.66 us (3%)
    pallas_call x1, Pallas kernels, shards(): pl.pallas_call(functools.partial(kernel, wide_count, narrow_count), out_s...  21.1 us
    unnamed x8, local copies, waits for them, and re-layouts  1.98 us
    reshape x1, local copies, waits for them, and re-layouts, shards(): q = jnp.transpose(q.reshape(3, radial, snaps, nodes), (2, 0, 1, 3))  1.76 us
    reshape x1, local copies, waits for them, and re-layouts, shards(): extents.reshape(3 * radial)  0.6 us

profile of v2, /device:TPU:0, one launch (start us, length us, event | category | flops | bytes accessed | tf_op | source)
XLA Modules:
  0.0 26.1 jit_solution(8229145739988675616)
XLA Ops:
  0.6 0.0 copy-start.2
  0.6 0.7 %copy-done.2 = f32[3,1,1,4]{3,2,1,0:T(1,128)S(1)} copy-done((f32[3,1,1,4]{3,2,1,0:T(1,128)S(1)}, f32[3,1,1,4]{3,2,1,0:T(1,128)}, u32[]{:S(2)}) %copy-start.2) | copy-done | bytes 72
  1.3 0.6 %reshape.19.ext_in = f32[12]{0:T(128)} reshape(f32[3,4]{1,0:T(4,128)S(1)} %reduce) | data formatting | bytes 96 | tf_op jit(solution)/shard_map/reshape | solution.py:484
  1.9 21.1 %pipe.1 = (bf16[192,512]{1,0:T(8,128)(2,1)}, f32[16,16]{1,0:T(8,128)}, f32[16,15]{1,0:T(8,128)}) custom-call(bf16[16,3,4,512]{3,2,1,0:T(4,128)(2,1)} %bitcast.7, f32[12]{0:T(128)} %reshape.19.ext_in, bf16[512,512]{1,0:T(8,128)(2,1)} %constant.10.clone.first_in, bf16[2,256,256]{2,1,0:T(8,128)(2,1)} %constant.11.clone.near_in, ...), custom_call_target="tpu_custom_call" | custom-call | flops 400000000 | bytes 3000000 | tf_op jit(solution)/shard_map/pipe/pallas_call | solution.py:491
  23.0 0.0 copy-start.1
  23.0 1.8 %copy.12 = bf16[3,4,16,512]{3,1,0,2:T(4,128)(2,1)} copy(bf16[3,4,16,512]{3,2,1,0:T(8,128)(2,1)} %bitcast.8) | data formatting | bytes 393216 | tf_op jit(solution)/shard_map/reshape | solution.py:534
  24.8 0.0 copy-done.1
  24.8 0.0 copy-start
  24.8 0.6 %copy.15 = f32[16,16]{1,0:T(8,128)} copy(f32[16,16]{1,0:T(8,128)S(1)} %copy-done.1) | data formatting | bytes 2048
  25.4 0.1 copy-done
  25.5 0.6 %copy.16 = f32[16,15]{1,0:T(8,128)} copy(f32[16,15]{1,0:T(8,128)S(1)} %copy-done) | data formatting | bytes 1920
  (1 shorter events, 0.0 us)
Async XLA Ops:
  0.6 0.7 %copy-start.2 = (f32[3,1,1,4]{3,2,1,0:T(1,128)S(1)}, f32[3,1,1,4]{3,2,1,0:T(1,128)}, u32[]{:S(2)}) copy-start(f32[3,1,1,4]{3,2,1,0:T(1,128)} %param.8) | copy-start | bytes 148
  23.0 1.8 %copy-start.1 = (f32[16,16]{1,0:T(8,128)S(1)}, f32[16,16]{1,0:T(8,128)}, u32[]{:S(2)}) copy-start(f32[16,16]{1,0:T(8,128)} %get-tuple-element.13) | copy-start | bytes 3076
  24.8 0.7 %copy-start = (f32[16,15]{1,0:T(8,128)S(1)}, f32[16,15]{1,0:T(8,128)}, u32[]{:S(2)}) copy-start(f32[16,15]{1,0:T(8,128)} %get-tuple-element.14) | copy-start | bytes 2884

commit v3 on v2

--- a/solution.py
+++ b/solution.py
@@ -77,6 +77,7 @@
         half(faces),
         half(spread),
         root,
+        np.concatenate([root[:, picks[:64]]] * 2, axis=1),
     )
 
 
@@ -100,9 +101,9 @@
     face_in,
     spread_in,
     root_in,
-    q_ref,
-    r_ref,
-    dmd_ref,
+    edge_root_in,
+    z_out,
+    total_ref,
     vel_ref,
     ext_ref,
     first_ref,
@@ -110,9 +111,12 @@
     face_ref,
     spread_ref,
     root_ref,
+    edge_root_ref,
     load_sem,
     rows_ref,
     vb_ref,
+    z_ref,
+    z_sem,
     send_narrow,
     recv_narrow,
     send_wide,
@@ -135,7 +139,6 @@
     fields = 3 * radial
     blocks = fields + 2 - fields % 2
     pairs = blocks // 2
-    row_count = fields * nodes * wide_count * narrow_count
     me_w, me_n = lax.axis_index("wide"), lax.axis_index("narrow")
     wide_at = lambda step: (lax.rem(me_w + step, wide_count), me_n)
     narrow_at = lambda step: (me_w, lax.rem(me_n + step, narrow_count))
@@ -151,6 +154,7 @@
                 (near_in, near_ref),
                 (spread_in, spread_ref),
                 (root_in, root_ref),
+                (edge_root_in, edge_root_ref),
             ]
         )
     ]
@@ -194,7 +198,7 @@
     ]
 
     loads[1].wait()
-    extent = [[ext_ref[k * radial + e] for e in range(radial)] for k in range(3)]
+    extent = [[ext_ref[k, 0, 0, e] for e in range(radial)] for k in range(3)]
     volume = [extent[0][e] * extent[1][e] * extent[2][e] for e in range(radial)]
 
     def curl(grads):
@@ -346,55 +350,88 @@
 
     edge_low, edge_high = residue == 0, residue == 7
 
-    def with_edges(way, p):
+    for copy in narrow_copies:
+        copy.wait()
+    highs, lows = [], []
+    for part_of in range(2):
+        for p in range(pairs):
+            below, above = recv_narrow[0, p], recv_narrow[1, p]
+            if part_of == 0:
+                both = jnp.where(left, below, pltpu.roll(above, 64, 1))
+            else:
+                both = jnp.where(left, pltpu.roll(below, 64, 1), above)
+            high, low = split(both)
+            highs.append(high)
+            lows.append(low)
+    stacked = jnp.concatenate(
+        [jnp.concatenate(highs, axis=0), jnp.concatenate(lows, axis=0)], axis=1
+    )
+    extra = dot(stacked, spread_ref[1])
+    field = [value + extra[b * snaps : (b + 1) * snaps] for b, value in enumerate(field)]
+    inner = jnp.logical_and(long_lane % 8 != 0, long_lane % 8 != 7)
+    scale = jnp.where(inner, root / field[fields], 0.0)
+    for b in range(fields):
+        e = b % radial
+        high, low = split(field[b] * scale[e : e + 1, :])
+        z_ref[0:snaps, pl.ds(b * nodes, nodes)] = high
+        z_ref[snaps : 2 * snaps, pl.ds(b * nodes, nodes)] = low
+
+    def products(both):
+        return lax.dot_general(
+            both, both, (((1,), (1,)), ((), ())), preferred_element_type=F32
+        )
+
+    inside = products(z_ref[...])
+    own = [[], []]
+    for p in range(pairs):
+        below, above = recv_narrow[0, p], recv_narrow[1, p]
+        own[0].append(
+            send_wide[1, p]
+            + jnp.where(edge_low, below, 0.0)
+            + jnp.where(edge_high, pltpu.roll(above, 7, 1), 0.0)
+        )
+        own[1].append(
+            send_wide[0, p]
+            + jnp.where(edge_high, above, 0.0)
+            + jnp.where(edge_low, pltpu.roll(below, 121, 1), 0.0)
+        )
+    edge_size = jnp.zeros((snaps, 128), F32)
+    for e in range(radial):
+        edge_size = jnp.where(line == e, jnp.full((snaps, 128), volume[e], F32), edge_size)
+    edge_root = jnp.sqrt(edge_size) * edge_root_ref[...]
+
+    for copy in edge_copies + wide_copies:
+        copy.wait()
+
+    def arrived(way, p):
         g, r = p // 4, p % 4
         pieces = []
         for slot, places, shift in ((0, edge_low, 121), (len(turns) - 1, edge_high, 7)):
             piece = pltpu.roll(recv_edge[way, slot, g], (shift - 2 * r) % 128, 1)
             pieces.append(jnp.where(places, piece, 0.0))
-        return recv_wide[way, p] + (pieces[0] + pieces[1])
-
-    def spread(received, which):
-        highs, lows = [], []
-        for part_of in range(2):
-            for p in range(pairs):
-                below, above = received(0, p), received(1, p)
-                if part_of == 0:
-                    both = jnp.where(left, below, pltpu.roll(above, 64, 1))
-                else:
-                    both = jnp.where(left, pltpu.roll(below, 64, 1), above)
-                high, low = split(both)
-                highs.append(high)
-                lows.append(low)
-        stacked = jnp.concatenate(
-            [jnp.concatenate(highs, axis=0), jnp.concatenate(lows, axis=0)], axis=1
-        )
-        return dot(stacked, spread_ref[which])
-
-    for copy in narrow_copies:
-        copy.wait()
-    extra = spread(lambda way, p: recv_narrow[way, p], 1)
-    field = [value + extra[b * snaps : (b + 1) * snaps] for b, value in enumerate(field)]
-
-    for copy in edge_copies + wide_copies:
-        copy.wait()
-    extra = spread(with_edges, 0)
-    field = [value + extra[b * snaps : (b + 1) * snaps] for b, value in enumerate(field)]
-
-    scale = root / field[fields]
-    highs, lows = [], []
-    for b in range(fields):
-        e = b % radial
-        high, low = split(field[b] * scale[e : e + 1, :])
-        highs.append(high)
-        lows.append(low)
-    high = jnp.concatenate(highs, axis=1)
-    low = jnp.concatenate(lows, axis=1)
-    both = jnp.concatenate([high, low], axis=0)
-    product = lax.dot_general(
-        both, both, (((1,), (1,)), ((), ())), preferred_element_type=F32
-    )
-    gram_ref[:, : 2 * snaps] = product
+        return own[way][p] + (recv_wide[way, p] + (pieces[0] + pieces[1]))
+
+    mass_pair, mass_left = fields % pairs, fields < pairs
+    ends = [[], []]
+    for way in range(2):
+        values = [arrived(way, p) for p in range(pairs)]
+        mass = values[mass_pair]
+        turned = pltpu.roll(mass, 64, 1)
+        mass = jnp.where(left, mass, turned) if mass_left else jnp.where(left, turned, mass)
+        scale = edge_root / mass
+        for p in range(pairs):
+            one, two = p % radial, (p + pairs) % radial
+            factor = jnp.where(left, scale[one : one + 1, :], scale[two : two + 1, :])
+            if p >= fields:
+                factor = jnp.zeros_like(factor)
+            elif p + pairs >= fields:
+                factor = jnp.where(left, factor, 0.0)
+            ends[way].append(split(values[p] * factor))
+    ends = ends[0] + ends[1]
+    both = jnp.concatenate(
+        [jnp.concatenate([end[i] for end in ends], axis=1) for i in range(2)], axis=0
+    )
+    gram_ref[:, : 2 * snaps] = inside + products(both)
     product = gram_ref[...]
     top = product[:snaps]
     gram = top + pltpu.roll(top, 128 - snaps, 1) + product[snaps:]
@@ -408,7 +445,7 @@
         inside = jnp.logical_and(slim_lane >= g * snaps, slim_lane < (g + 1) * snaps)
         compact = jnp.where(inside, piece, compact)
 
-    def total(own, buffer, me, at, count, send_sem, recv_sem):
+    def total(own, buffer, me, at, count, send_sem, recv_sem, meanwhile=None):
         buffer[me] = own
         copies = [
             pltpu.make_async_remote_copy(
@@ -423,6 +460,8 @@
         ]
         for copy in copies:
             copy.start()
+        if meanwhile is not None:
+            meanwhile()
         for copy in copies:
             copy.wait()
         terms = [buffer[i] for i in range(count)]
@@ -436,20 +475,68 @@
     compact = total(
         compact, narrow_gram, me_n, narrow_at, narrow_count, narrow_send_sem, narrow_recv_sem
     )
-    compact = total(
-        compact, wide_gram, me_w, wide_at, wide_count, wide_send_sem, wide_recv_sem
-    )
-
+
+    def whole_rows():
+        for i in range(2):
+            values = []
+            for b in range(fields):
+                p, two = b % pairs, b >= pairs
+                low, high = ends[p][i].astype(F32), ends[pairs + p][i].astype(F32)
+                if two:
+                    low = pltpu.roll(low, 64, 1)
+                else:
+                    high = pltpu.roll(high, 64, 1)
+                values.append(jnp.where(left, low, high))
+            rows = dot(jnp.concatenate(values, axis=0).astype(BF16), spread_ref[0, 0:128, :])
+            for b in range(fields):
+                at = (pl.ds(i * snaps, snaps), pl.ds(b * nodes, nodes))
+                kept = z_ref[at].astype(F32)
+                z_ref[at] = (kept + rows[b * snaps : (b + 1) * snaps]).astype(BF16)
+        copy = pltpu.make_async_copy(z_ref, z_out, z_sem)
+        copy.start()
+        return copy
+
+    copy = []
+    total_ref[...] = total(
+        compact,
+        wide_gram,
+        me_w,
+        wide_at,
+        wide_count,
+        wide_send_sem,
+        wide_recv_sem,
+        lambda: copy.append(whole_rows()),
+    )
+    copy[0].wait()
+
+
+def basis_kernel(
+    row_count, radial, total_ref, z_in, q_ref, r_ref, dmd_ref, z_ref, rows_ref, z_sem
+):
+    snaps, nodes = q_ref.shape[0], q_ref.shape[3]
+    fields = 3 * radial
+    load = pltpu.make_async_copy(z_in, z_ref, z_sem)
+    load.start()
+    lane = lax.broadcasted_iota(jnp.int32, (snaps, 128), 1)
+    line = lax.broadcasted_iota(jnp.int32, (snaps, 128), 0)
+    compact = total_ref[...]
     lines = [compact]
-    for g in range(1, groups):
+    for g in range(1, snaps // 8):
         lines.append(pltpu.roll(compact, 128 - g * snaps, 1))
     work = jnp.concatenate(lines, axis=0)
     unit = jnp.logical_and(lane % snaps == line, lane < 4 * snaps)
     work = jnp.where(lane < snaps, work, jnp.where(unit, 1.0, 0.0))
-    for k in range(snaps - 1):
-        lead = work[k : k + 1, :]
-        ratio = lead * (1.0 / work[k : k + 1, k : k + 1])
-        work = work - jnp.where(line > k, work[:, k : k + 1], 0.0) * ratio
+    for k in range(0, snaps - 1, 2):
+        row_a, row_b = work[k : k + 1, :], work[k + 1 : k + 2, :]
+        col_a, col_b = work[:, k : k + 1], work[:, k + 1 : k + 2]
+        inv_a = 1.0 / work[k : k + 1, k : k + 1]
+        cross = work[k : k + 1, k + 1 : k + 2]
+        ratio = cross * inv_a
+        inv_b = 1.0 / (work[k + 1 : k + 2, k + 1 : k + 2] - cross * ratio)
+        row_b = row_b - ratio * row_a
+        col_b = col_b - ratio * col_a
+        after = work - col_a * (inv_a * row_a) - col_b * (inv_b * row_b)
+        work = jnp.where(line > k + 1, after, jnp.where(line == k + 1, row_b, work))
     pivot = jnp.sum(jnp.where(lane == line, work, 0.0), axis=1, keepdims=True)
     work = work * (1.0 / jnp.sqrt(pivot))
     norm = math.sqrt(row_count)
@@ -457,9 +544,18 @@
     big, small = split(inverse * norm)
     weights = jnp.where(lane < 2 * snaps, big.astype(F32), small.astype(F32))
     weights = weights[:, : 3 * snaps].astype(BF16)
-    basis = dot(weights, jnp.concatenate([both, high], axis=0))
+    load.wait()
+    basis = dot(weights, jnp.concatenate([z_ref[...], z_ref[0:snaps, :]], axis=0))
     for b in range(fields):
-        q_ref[pl.ds(b * snaps, snaps), :] = basis[:, b * nodes : (b + 1) * nodes].astype(BF16)
+        for j in range(nodes // 128):
+            first = b * nodes + 128 * j
+            rows_ref[j, pl.ds(b, snaps, stride=fields), :] = basis[:, first : first + 128]
+    for s in range(snaps):
+        for c in range(3):
+            value = [
+                rows_ref[j, pl.ds((s * 3 + c) * radial, radial), :] for j in range(nodes // 128)
+            ]
+            q_ref[s, c] = jnp.concatenate(value, axis=1).astype(BF16)
     upper = jnp.where(jnp.logical_and(lane >= line, lane < snaps), work, 0.0)
     r_ref[...] = upper[:, :snaps] / norm
     moved = jnp.where(lane < snaps - 1, pltpu.roll(upper, 127, 1), 0.0)
@@ -481,22 +577,21 @@
     vmem = pl.BlockSpec(memory_space=pltpu.VMEM)
     operands = [
         velocity.reshape(snaps, 3, radial, nodes),
-        extents.reshape(3 * radial),
+        extents,
         *[jnp.asarray(table) for table in tables()],
     ]
     corners = len({1, narrow_count - 1})
     edge = (-(-pairs // 4), snaps, 128)
     face = pltpu.VMEM((2, pairs, snaps, 128), F32)
     dma = pltpu.SemaphoreType.DMA
-    q, r, dmd = pl.pallas_call(
+    limit = 60 * 1024 * 1024
+    hbm = pl.BlockSpec(memory_space=pltpu.HBM)
+    rows = jax.ShapeDtypeStruct((2 * snaps, fields * nodes), BF16)
+    rows, total = pl.pallas_call(
         functools.partial(kernel, wide_count, narrow_count),
-        out_shape=(
-            jax.ShapeDtypeStruct((fields * snaps, nodes), BF16),
-            jax.ShapeDtypeStruct((snaps, snaps), F32),
-            jax.ShapeDtypeStruct((snaps, snaps - 1), F32),
-        ),
-        in_specs=[pl.BlockSpec(memory_space=pltpu.HBM)] * len(operands),
-        out_specs=(vmem, vmem, vmem),
+        out_shape=(rows, jax.ShapeDtypeStruct((8, 128), F32)),
+        in_specs=[hbm] * len(operands),
+        out_specs=(hbm, vmem),
         scratch_shapes=[
             (pltpu.SMEM if i == 1 else pltpu.VMEM)(operand.shape, operand.dtype)
             for i, operand in enumerate(operands)
@@ -505,6 +600,8 @@
             dma((len(operands),)),
             pltpu.VMEM((nodes // 128, fields * snaps, 128), F32),
             pltpu.VMEM((fields * snaps, nodes), BF16),
+            pltpu.VMEM((2 * snaps, fields * nodes), BF16),
+            dma(()),
             face,
             face,
             face,
@@ -524,14 +621,31 @@
             dma((wide_count - 1,)),
         ],
         compiler_params=pltpu.CompilerParams(
-            collective_id=0, has_side_effects=True, vmem_limit_bytes=60 * 1024 * 1024
+            collective_id=0, has_side_effects=True, vmem_limit_bytes=limit
         ),
         cost_estimate=pl.CostEstimate(
             flops=400_000_000, bytes_accessed=3_000_000, transcendentals=10_000
         ),
         name="pipe",
     )(*operands)
-    q = jnp.transpose(q.reshape(3, radial, snaps, nodes), (2, 0, 1, 3))
+    row_count = fields * nodes * wide_count * narrow_count
+    q, r, dmd = pl.pallas_call(
+        functools.partial(basis_kernel, row_count, radial),
+        out_shape=(
+            jax.ShapeDtypeStruct((snaps, 3, radial, nodes), BF16),
+            jax.ShapeDtypeStruct((snaps, snaps), F32),
+            jax.ShapeDtypeStruct((snaps, snaps - 1), F32),
+        ),
+        in_specs=[vmem, hbm],
+        out_specs=(vmem, vmem, vmem),
+        scratch_shapes=[
+            pltpu.VMEM((2 * snaps, fields * nodes), BF16),
+            pltpu.VMEM((nodes // 128, fields * snaps, 128), F32),
+            dma(()),
+        ],
+        compiler_params=pltpu.CompilerParams(vmem_limit_bytes=limit),
+        name="basis",
+    )(total, rows)
     return q.reshape(velocity.shape), r, dmd
 
 

time: 26.3 us -> 23.2 us (0.88)
  local copies, waits for them, and re-layouts: 4.34 us -> 0 us
  Pallas kernels: 21.1 us -> 22.4 us
    pallas_call x0 -> x1, Pallas kernels: none -> 3.04 us  [shards(): pl.pallas_call(functools.partial(basis_kernel, row_count, radial), out_sh...]
    reshape x2 -> x0, local copies, waits for them, and re-layouts: 2.36 us -> none  [the longest x1 1.76 us: shards(): q = jnp.transpose(q.reshape(3, radial, snaps, nodes), (2, 0, 1, 3))]
    unnamed x8 -> x0, local copies, waits for them, and re-layouts: 1.98 us -> none
    pallas_call x1, Pallas kernels: 21.1 us -> 19.3 us  [shards(): pl.pallas_call(functools.partial(kernel, wide_count, narrow_count), out_s...]
where the time goes in v3:
time: 23.2 us; the launch traced here: 23 us
  Pallas kernels  22.4 us (97%)
  between operations  0.64 us (3%)
    pallas_call x1, Pallas kernels, shards(): pl.pallas_call(functools.partial(kernel, wide_count, narrow_count), out_s...  19.3 us
    pallas_call x1, Pallas kernels, shards(): pl.pallas_call(functools.partial(basis_kernel, row_count, radial), out_sh...  3.04 us

profile of v3, /device:TPU:0, one launch (start us, length us, event | category | flops | bytes accessed | tf_op | source)
XLA Modules:
  0.0 23.0 jit_solution(16403866975114797772)
XLA Ops:
  0.6 19.3 %pipe.1 = (bf16[32,6144]{1,0:T(8,128)(2,1)}, f32[8,128]{1,0:T(8,128)}) custom-call(bf16[16,3,4,512]{3,2,1,0:T(4,128)(2,1)} %bitcast.4, f32[3,1,1,4]{3,2,1,0:T(1,128)} %ext_in.1, bf16[512,512]{1,0:T(8,128)(2,1)} %constant.12.clone.first_in, bf16[2,256,256]{2,1,0:T(8,128)(2,1)} %constant.13.clone.near_in, bf16[1536,256]{1,0:T(8,128)(2,1)} %constant.14.clone.face_in, ...), custom_call_target="tpu_custom_call" | custom-call | flops 400000000 | bytes 3000000 | tf_op jit(solution)/shard_map/pipe/pallas_call | solution.py:590
  20.0 3.0 %basis.1 = (bf16[16,3,4,512]{3,2,1,0:T(4,128)(2,1)}, f32[16,16]{1,0:T(8,128)}, f32[16,15]{1,0:T(8,128)}) custom-call(f32[8,128]{1,0:T(8,128)} %get-tuple-element.8.total_ref, bf16[32,6144]{1,0:T(8,128)(2,1)} %get-tuple-element.9.z_in), custom_call_target="tpu_custom_call" | custom-call | tf_op jit(solution)/shard_map/basis/pallas_call | solution.py:632

commit v4 on v3

--- a/solution.py
+++ b/solution.py
@@ -124,16 +124,13 @@
     send_edge,
     recv_edge,
     gram_ref,
-    narrow_gram,
-    wide_gram,
+    sums_ref,
     face_send_sem,
     face_recv_sem,
     edge_send_sem,
     edge_recv_sem,
-    narrow_send_sem,
-    narrow_recv_sem,
-    wide_send_sem,
-    wide_recv_sem,
+    sum_send_sem,
+    sum_recv_sem,
 ):
     snaps, _, radial, nodes = vel_ref.shape
     fields = 3 * radial
@@ -158,25 +155,35 @@
             ]
         )
     ]
-    for load in loads:
+    for load in loads[:3]:
         load.start()
 
     barrier = pltpu.get_barrier_semaphore()
-    for step in range(1, narrow_count):
-        pl.semaphore_signal(barrier, inc=1, device_id=narrow_at(step), device_id_type=MESH)
-    for step in range(1, wide_count):
-        pl.semaphore_signal(barrier, inc=1, device_id=wide_at(step), device_id_type=MESH)
+    count = wide_count * narrow_count
+    me = me_w * narrow_count + me_n
+
+    def device(step):
+        peer = lax.rem(me + step, count)
+        return (peer // narrow_count, lax.rem(peer, narrow_count))
+
+    def each_peer(action):
+        if count <= 64:
+            for step in range(1, count):
+                action(step)
+        else:
+            lax.fori_loop(1, count, lambda step, carry: (action(step), carry)[1], 0)
+
+    each_peer(
+        lambda step: pl.semaphore_signal(
+            barrier, inc=1, device_id=device(step), device_id_type=MESH
+        )
+    )
     turns = sorted({1, narrow_count - 1})
     corner_at = lambda step, turn: (
         lax.rem(me_w + step, wide_count),
         lax.rem(me_n + turn, narrow_count),
     )
     ways = (1, wide_count - 1)
-    for step in ways:
-        for turn in turns:
-            pl.semaphore_signal(
-                barrier, inc=1, device_id=corner_at(step, turn), device_id_type=MESH
-            )
     loads[0].wait()
     for s in range(snaps):
         for c in range(3):
@@ -213,6 +220,8 @@
         return out
 
     loads[2].wait()
+    for load in loads[3:]:
+        load.start()
     grads = [dot(pair[k], face_ref[pl.ds(k * nodes, nodes), :]) for k in range(3)]
     raw = curl(grads)
     lane = lax.broadcasted_iota(jnp.int32, (snaps, 128), 1)
@@ -251,10 +260,6 @@
         high = jnp.where(left, pltpu.roll(one, 64, 1), two)
         return low, high
 
-    for p in range(pairs):
-        low, high = packed(1, p)
-        send_narrow[0, p] = high
-        send_narrow[1, p] = low
     groups_of = -(-pairs // 4)
     residue = lane % 8
     edge_of = [
@@ -276,7 +281,7 @@
         for way in range(2):
             send_edge[way, g] = edges[way]
 
-    pl.semaphore_wait(barrier, wide_count + narrow_count - 2 + 2 * len(turns))
+    pl.semaphore_wait(barrier, count - 1)
 
     def face_copies(source, target, at, count, first):
         return [
@@ -304,8 +309,14 @@
         for way in range(2)
         for i, turn in enumerate(turns)
     ]
+    for copy in wide_copies + edge_copies:
+        copy.start()
+    for p in range(pairs):
+        low, high = packed(1, p)
+        send_narrow[0, p] = high
+        send_narrow[1, p] = low
     narrow_copies = face_copies(send_narrow, recv_narrow, narrow_at, narrow_count, 0)
-    for copy in wide_copies + edge_copies + narrow_copies:
+    for copy in narrow_copies:
         copy.start()
 
     for load in loads[3:]:
@@ -435,46 +446,23 @@
     product = gram_ref[...]
     top = product[:snaps]
     gram = top + pltpu.roll(top, 128 - snaps, 1) + product[snaps:]
-    slim_lane = lax.broadcasted_iota(jnp.int32, (8, 128), 1)
+    gram = jnp.where(lane < snaps, gram, 0.0)
     groups = snaps // 8
-    compact = jnp.zeros((8, 128), F32)
     for g in range(groups):
-        piece = gram[8 * g : 8 * g + 8]
-        if g:
-            piece = pltpu.roll(piece, g * snaps, 1)
-        inside = jnp.logical_and(slim_lane >= g * snaps, slim_lane < (g + 1) * snaps)
-        compact = jnp.where(inside, piece, compact)
-
-    def total(own, buffer, me, at, count, send_sem, recv_sem, meanwhile=None):
-        buffer[me] = own
-        copies = [
-            pltpu.make_async_remote_copy(
-                src_ref=buffer.at[me],
-                dst_ref=buffer.at[me],
-                send_sem=send_sem.at[step - 1],
-                recv_sem=recv_sem.at[step - 1],
-                device_id=at(step),
-                device_id_type=MESH,
-            )
-            for step in range(1, count)
-        ]
-        for copy in copies:
-            copy.start()
-        if meanwhile is not None:
-            meanwhile()
-        for copy in copies:
-            copy.wait()
-        terms = [buffer[i] for i in range(count)]
-        while len(terms) > 1:
-            terms = [
-                terms[i] + terms[i + 1] if i + 1 < len(terms) else terms[i]
-                for i in range(0, len(terms), 2)
-            ]
-        return terms[0]
-
-    compact = total(
-        compact, narrow_gram, me_n, narrow_at, narrow_count, narrow_send_sem, narrow_recv_sem
-    )
+        piece = pltpu.roll(gram[8 * g : 8 * g + 8], 0, 1, stride=snaps, stride_axis=0)
+        sums_ref[me, g : g + 1, :] = jnp.sum(piece, axis=0, keepdims=True)
+
+    def sum_copy(step):
+        return pltpu.make_async_remote_copy(
+            src_ref=sums_ref.at[me],
+            dst_ref=sums_ref.at[me],
+            send_sem=sum_send_sem,
+            recv_sem=sum_recv_sem,
+            device_id=device(step),
+            device_id_type=MESH,
+        )
+
+    each_peer(lambda step: sum_copy(step).start())
 
     def whole_rows():
         for i in range(2):
@@ -496,18 +484,18 @@
         copy.start()
         return copy
 
-    copy = []
-    total_ref[...] = total(
-        compact,
-        wide_gram,
-        me_w,
-        wide_at,
-        wide_count,
-        wide_send_sem,
-        wide_recv_sem,
-        lambda: copy.append(whole_rows()),
-    )
-    copy[0].wait()
+    copy = whole_rows()
+    others = sums_ref.at[pl.ds(0, count - 1)]
+    pltpu.make_async_copy(others, others, sum_recv_sem).wait()
+    pltpu.make_async_copy(others, others, sum_send_sem).wait()
+    terms = [sums_ref[i] for i in range(count)]
+    while len(terms) > 1:
+        terms = [
+            terms[i] + terms[i + 1] if i + 1 < len(terms) else terms[i]
+            for i in range(0, len(terms), 2)
+        ]
+    total_ref[...] = terms[0]
+    copy.wait()
 
 
 def basis_kernel(
@@ -519,10 +507,13 @@
     load.start()
     lane = lax.broadcasted_iota(jnp.int32, (snaps, 128), 1)
     line = lax.broadcasted_iota(jnp.int32, (snaps, 128), 0)
-    compact = total_ref[...]
-    lines = [compact]
-    for g in range(1, snaps // 8):
-        lines.append(pltpu.roll(compact, 128 - g * snaps, 1))
+    lines = []
+    for g in range(snaps // 8):
+        whole = jnp.broadcast_to(total_ref[g : g + 1, :], (8, 128))
+        piece = whole
+        for i in range(1, 8):
+            piece = jnp.where(line[:8] == i, pltpu.roll(whole, 128 - snaps * i, 1), piece)
+        lines.append(piece)
     work = jnp.concatenate(lines, axis=0)
     unit = jnp.logical_and(lane % snaps == line, lane < 4 * snaps)
     work = jnp.where(lane < snaps, work, jnp.where(unit, 1.0, 0.0))
@@ -589,7 +580,7 @@
     rows = jax.ShapeDtypeStruct((2 * snaps, fields * nodes), BF16)
     rows, total = pl.pallas_call(
         functools.partial(kernel, wide_count, narrow_count),
-        out_shape=(rows, jax.ShapeDtypeStruct((8, 128), F32)),
+        out_shape=(rows, jax.ShapeDtypeStruct((snaps // 8, 128), F32)),
         in_specs=[hbm] * len(operands),
         out_specs=(hbm, vmem),
         scratch_shapes=[
@@ -609,16 +600,13 @@
             pltpu.VMEM((2,) + edge, F32),
             pltpu.VMEM((2, corners) + edge, F32),
             pltpu.VMEM((2 * snaps, 128), F32),
-            pltpu.VMEM((narrow_count, 8, 128), F32),
-            pltpu.VMEM((wide_count, 8, 128), F32),
+            pltpu.VMEM((wide_count * narrow_count, snaps // 8, 128), F32),
             dma((4,)),
             dma((4,)),
             dma((2, corners)),
             dma((2, corners)),
-            dma((narrow_count - 1,)),
-            dma((narrow_count - 1,)),
-            dma((wide_count - 1,)),
-            dma((wide_count - 1,)),
+            dma(()),
+            dma(()),
         ],
         compiler_params=pltpu.CompilerParams(
             collective_id=0, has_side_effects=True, vmem_limit_bytes=limit

time: 23.2 us -> 22 us (0.948)
  Pallas kernels: 22.4 us -> 21.2 us
    pallas_call x1, Pallas kernels: 19.3 us -> 18.1 us  [shards(): pl.pallas_call(functools.partial(kernel, wide_count, narrow_count), out_s...]
where the time goes in v4:
time: 22 us; the launch traced here: 21.9 us
  Pallas kernels  21.2 us (96%)
  between operations  0.64 us (3%)
    pallas_call x1, Pallas kernels, shards(): pl.pallas_call(functools.partial(kernel, wide_count, narrow_count), out_s...  18.1 us
    pallas_call x1, Pallas kernels, shards(): pl.pallas_call(functools.partial(basis_kernel, row_count, radial), out_sh...  3.11 us

profile of v4, /device:TPU:0, one launch (start us, length us, event | category | flops | bytes accessed | tf_op | source)
XLA Modules:
  0.0 21.9 jit_solution(5781855873381668513)
XLA Ops:
  0.6 18.1 %pipe.1 = (bf16[32,6144]{1,0:T(8,128)(2,1)}, f32[2,128]{1,0:T(2,128)}) custom-call(bf16[16,3,4,512]{3,2,1,0:T(4,128)(2,1)} %bitcast.4, f32[3,1,1,4]{3,2,1,0:T(1,128)} %ext_in.1, bf16[512,512]{1,0:T(8,128)(2,1)} %constant.12.clone.first_in, bf16[2,256,256]{2,1,0:T(8,128)(2,1)} %constant.13.clone.near_in, bf16[1536,256]{1,0:T(8,128)(2,1)} %constant.14.clone.face_in, ...), custom_call_target="tpu_custom_call" | custom-call | flops 400000000 | bytes 3000000 | tf_op jit(solution)/shard_map/pipe/pallas_call | solution.py:581
  18.7 3.1 %basis.1 = (bf16[16,3,4,512]{3,2,1,0:T(4,128)(2,1)}, f32[16,16]{1,0:T(8,128)}, f32[16,15]{1,0:T(8,128)}) custom-call(f32[2,128]{1,0:T(2,128)} %get-tuple-element.8.total_ref, bf16[32,6144]{1,0:T(8,128)(2,1)} %get-tuple-element.9.z_in), custom_call_target="tpu_custom_call" | custom-call | tf_op jit(solution)/shard_map/basis/pallas_call | solution.py:620

commit v5 on v4

--- a/solution.py
+++ b/solution.py
@@ -137,8 +137,15 @@
     blocks = fields + 2 - fields % 2
     pairs = blocks // 2
     me_w, me_n = lax.axis_index("wide"), lax.axis_index("narrow")
-    wide_at = lambda step: (lax.rem(me_w + step, wide_count), me_n)
-    narrow_at = lambda step: (me_w, lax.rem(me_n + step, narrow_count))
+    wrapped = lambda place, size: jnp.where(place >= size, place - size, place)
+    wide_at = lambda step: (wrapped(me_w + step, wide_count), me_n)
+    narrow_at = lambda step: (me_w, wrapped(me_n + step, narrow_count))
+    turns = sorted({1, narrow_count - 1})
+    corner_at = lambda step, turn: (
+        wrapped(me_w + step, wide_count),
+        wrapped(me_n + turn, narrow_count),
+    )
+    ways = (1, wide_count - 1)
 
     loads = [
         pltpu.make_async_copy(source, target, load_sem.at[i])
@@ -162,28 +169,27 @@
     count = wide_count * narrow_count
     me = me_w * narrow_count + me_n
 
-    def device(step):
-        peer = lax.rem(me + step, count)
-        return (peer // narrow_count, lax.rem(peer, narrow_count))
-
     def each_peer(action):
+        steps = sorted(range(wide_count), key=lambda step: abs(2 * step - wide_count))
         if count <= 64:
-            for step in range(1, count):
-                action(step)
+            for step in steps:
+                for turn in range(narrow_count):
+                    if step or turn:
+                        action(corner_at(step, turn))
         else:
-            lax.fori_loop(1, count, lambda step, carry: (action(step), carry)[1], 0)
+
+            def one_step(step, carry):
+                for turn in range(narrow_count):
+                    action(corner_at(step, turn))
+                return carry
+
+            lax.fori_loop(1, wide_count, one_step, 0)
+            for turn in range(1, narrow_count):
+                action(narrow_at(turn))
 
     each_peer(
-        lambda step: pl.semaphore_signal(
-            barrier, inc=1, device_id=device(step), device_id_type=MESH
-        )
+        lambda peer: pl.semaphore_signal(barrier, inc=1, device_id=peer, device_id_type=MESH)
     )
-    turns = sorted({1, narrow_count - 1})
-    corner_at = lambda step, turn: (
-        lax.rem(me_w + step, wide_count),
-        lax.rem(me_n + turn, narrow_count),
-    )
-    ways = (1, wide_count - 1)
     loads[0].wait()
     for s in range(snaps):
         for c in range(3):
@@ -452,17 +458,17 @@
         piece = pltpu.roll(gram[8 * g : 8 * g + 8], 0, 1, stride=snaps, stride_axis=0)
         sums_ref[me, g : g + 1, :] = jnp.sum(piece, axis=0, keepdims=True)
 
-    def sum_copy(step):
+    def sum_copy(peer):
         return pltpu.make_async_remote_copy(
             src_ref=sums_ref.at[me],
             dst_ref=sums_ref.at[me],
             send_sem=sum_send_sem,
             recv_sem=sum_recv_sem,
-            device_id=device(step),
+            device_id=peer,
             device_id_type=MESH,
         )
 
-    each_peer(lambda step: sum_copy(step).start())
+    each_peer(lambda peer: sum_copy(peer).start())
 
     def whole_rows():
         for i in range(2):

time: 22 us -> 22.4 us (1.018)
  Pallas kernels: 21.2 us -> 21.6 us
    pallas_call x1, Pallas kernels: 18.1 us -> 18.5 us  [shards(): pl.pallas_call(functools.partial(kernel, wide_count, narrow_count), out_s...]
where the time goes in v5:
time: 22.4 us; the launch traced here: 22.2 us
  Pallas kernels  21.6 us (96%)
  between operations  0.64 us (3%)
    pallas_call x1, Pallas kernels, shards(): pl.pallas_call(functools.partial(kernel, wide_count, narrow_count), out_s...  18.5 us
    pallas_call x1, Pallas kernels, shards(): pl.pallas_call(functools.partial(basis_kernel, row_count, radial), out_sh...  3.11 us

profile of v5, /device:TPU:0, one launch (start us, length us, event | category | flops | bytes accessed | tf_op | source)
XLA Modules:
  0.0 22.2 jit_solution(13041300995233343583)
XLA Ops:
  0.6 18.5 %pipe.1 = (bf16[32,6144]{1,0:T(8,128)(2,1)}, f32[2,128]{1,0:T(2,128)}) custom-call(bf16[16,3,4,512]{3,2,1,0:T(4,128)(2,1)} %bitcast.4, f32[3,1,1,4]{3,2,1,0:T(1,128)} %ext_in.1, bf16[512,512]{1,0:T(8,128)(2,1)} %constant.12.clone.first_in, bf16[2,256,256]{2,1,0:T(8,128)(2,1)} %constant.13.clone.near_in, bf16[1536,256]{1,0:T(8,128)(2,1)} %constant.14.clone.face_in, ...), custom_call_target="tpu_custom_call" | custom-call | flops 400000000 | bytes 3000000 | tf_op jit(solution)/shard_map/pipe/pallas_call | solution.py:587
  19.1 3.1 %basis.1 = (bf16[16,3,4,512]{3,2,1,0:T(4,128)(2,1)}, f32[16,16]{1,0:T(8,128)}, f32[16,15]{1,0:T(8,128)}) custom-call(f32[2,128]{1,0:T(2,128)} %get-tuple-element.8.total_ref, bf16[32,6144]{1,0:T(8,128)(2,1)} %get-tuple-element.9.z_in), custom_call_target="tpu_custom_call" | custom-call | tf_op jit(solution)/shard_map/basis/pallas_call | solution.py:626

commit v6 on v5

--- a/solution.py
+++ b/solution.py
@@ -123,7 +123,6 @@
     recv_wide,
     send_edge,
     recv_edge,
-    gram_ref,
     sums_ref,
     face_send_sem,
     face_recv_sem,
@@ -203,7 +202,6 @@
             vb_ref[pl.ds(b * snaps, snaps), pl.ds(128 * j, 128)] = rows_ref[
                 j, pl.ds(b, snaps, stride=fields), :
             ].astype(BF16)
-    gram_ref[...] = jnp.zeros_like(gram_ref)
     part = radial * snaps
     comp = lambda c: vb_ref[pl.ds(c * part, part), :]
     pair = [
@@ -390,15 +388,36 @@
     for b in range(fields):
         e = b % radial
         high, low = split(field[b] * scale[e : e + 1, :])
-        z_ref[0:snaps, pl.ds(b * nodes, nodes)] = high
-        z_ref[snaps : 2 * snaps, pl.ds(b * nodes, nodes)] = low
-
-    def products(both):
-        return lax.dot_general(
-            both, both, (((1,), (1,)), ((), ())), preferred_element_type=F32
-        )
-
-    inside = products(z_ref[...])
+        z_ref[b, 0:snaps, :] = high
+        z_ref[b, snaps : 2 * snaps, :] = low
+
+    def products(chunks):
+        size = 2 * snaps
+        stack = jnp.concatenate(chunks, axis=0)
+        grid = lax.dot_general(
+            stack, stack, (((1,), (1,)), ((), ())), preferred_element_type=F32
+        )
+        out = None
+        for i in range(len(chunks)):
+            first = i * size // 128 * 128
+            block = grid[i * size : (i + 1) * size, first : min(first + 128, grid.shape[1])]
+            if block.shape[1] < 128:
+                rest = jnp.zeros((size, 128 - block.shape[1]), F32)
+                block = jnp.concatenate([block, rest], axis=1)
+            if i * size > first:
+                block = pltpu.roll(block, 128 - (i * size - first), 1)
+            out = block if out is None else out + block
+        return out
+
+    at_once = max(1, 8 * fields // 48)
+    while fields % at_once:
+        at_once -= 1
+    inside = products(
+        [
+            jnp.concatenate([z_ref[b] for b in range(first, first + at_once)], axis=1)
+            for first in range(0, fields, at_once)
+        ]
+    )
     own = [[], []]
     for p in range(pairs):
         below, above = recv_narrow[0, p], recv_narrow[1, p]
@@ -445,11 +464,13 @@
                 factor = jnp.where(left, factor, 0.0)
             ends[way].append(split(values[p] * factor))
     ends = ends[0] + ends[1]
-    both = jnp.concatenate(
-        [jnp.concatenate([end[i] for end in ends], axis=1) for i in range(2)], axis=0
-    )
-    gram_ref[:, : 2 * snaps] = inside + products(both)
-    product = gram_ref[...]
+    stacks = [jnp.concatenate(end, axis=0) for end in ends]
+    product = inside + products(
+        [
+            jnp.concatenate(stacks[first : first + 2], axis=1)
+            for first in range(0, len(stacks), 2)
+        ]
+    )
     top = product[:snaps]
     gram = top + pltpu.roll(top, 128 - snaps, 1) + product[snaps:]
     gram = jnp.where(lane < snaps, gram, 0.0)
@@ -483,7 +504,7 @@
                 values.append(jnp.where(left, low, high))
             rows = dot(jnp.concatenate(values, axis=0).astype(BF16), spread_ref[0, 0:128, :])
             for b in range(fields):
-                at = (pl.ds(i * snaps, snaps), pl.ds(b * nodes, nodes))
+                at = (b, pl.ds(i * snaps, snaps), slice(None))
                 kept = z_ref[at].astype(F32)
                 z_ref[at] = (kept + rows[b * snaps : (b + 1) * snaps]).astype(BF16)
         copy = pltpu.make_async_copy(z_ref, z_out, z_sem)
@@ -542,11 +563,10 @@
     weights = jnp.where(lane < 2 * snaps, big.astype(F32), small.astype(F32))
     weights = weights[:, : 3 * snaps].astype(BF16)
     load.wait()
-    basis = dot(weights, jnp.concatenate([z_ref[...], z_ref[0:snaps, :]], axis=0))
     for b in range(fields):
+        basis = dot(weights, jnp.concatenate([z_ref[b], z_ref[b, 0:snaps, :]], axis=0))
         for j in range(nodes // 128):
-            first = b * nodes + 128 * j
-            rows_ref[j, pl.ds(b, snaps, stride=fields), :] = basis[:, first : first + 128]
+            rows_ref[j, pl.ds(b, snaps, stride=fields), :] = basis[:, 128 * j : 128 * j + 128]
     for s in range(snaps):
         for c in range(3):
             value = [
@@ -583,7 +603,7 @@
     dma = pltpu.SemaphoreType.DMA
     limit = 60 * 1024 * 1024
     hbm = pl.BlockSpec(memory_space=pltpu.HBM)
-    rows = jax.ShapeDtypeStruct((2 * snaps, fields * nodes), BF16)
+    rows = jax.ShapeDtypeStruct((fields, 2 * snaps, nodes), BF16)
     rows, total = pl.pallas_call(
         functools.partial(kernel, wide_count, narrow_count),
         out_shape=(rows, jax.ShapeDtypeStruct((snaps // 8, 128), F32)),
@@ -597,7 +617,7 @@
             dma((len(operands),)),
             pltpu.VMEM((nodes // 128, fields * snaps, 128), F32),
             pltpu.VMEM((fields * snaps, nodes), BF16),
-            pltpu.VMEM((2 * snaps, fields * nodes), BF16),
+            pltpu.VMEM((fields, 2 * snaps, nodes), BF16),
             dma(()),
             face,
             face,
@@ -605,7 +625,6 @@
             face,
             pltpu.VMEM((2,) + edge, F32),
             pltpu.VMEM((2, corners) + edge, F32),
-            pltpu.VMEM((2 * snaps, 128), F32),
             pltpu.VMEM((wide_count * narrow_count, snaps // 8, 128), F32),
             dma((4,)),
             dma((4,)),
@@ -633,7 +652,7 @@
         in_specs=[vmem, hbm],
         out_specs=(vmem, vmem, vmem),
         scratch_shapes=[
-            pltpu.VMEM((2 * snaps, fields * nodes), BF16),
+            pltpu.VMEM((fields, 2 * snaps, nodes), BF16),
             pltpu.VMEM((nodes // 128, fields * snaps, 128), F32),
             dma(()),
         ],

time: 22.4 us -> 22.2 us (level)
  no operation moved by 1% of the time
where the time goes in v6:
time: 22.2 us; the launch traced here: 22.1 us
  Pallas kernels  21.4 us (96%)
  between operations  0.64 us (3%)
    pallas_call x1, Pallas kernels, shards(): pl.pallas_call(functools.partial(kernel, wide_count, narrow_count), out_s...  18.3 us
    pallas_call x1, Pallas kernels, shards(): pl.pallas_call(functools.partial(basis_kernel, row_count, radial), out_sh...  3.11 us

profile of v6, /device:TPU:0, one launch (start us, length us, event | category | flops | bytes accessed | tf_op | source)
XLA Modules:
  0.0 22.1 jit_solution(3292041571274570165)
XLA Ops:
  0.6 18.3 %pipe.1 = (bf16[12,32,512]{2,1,0:T(8,128)(2,1)}, f32[2,128]{1,0:T(2,128)}) custom-call(bf16[16,3,4,512]{3,2,1,0:T(4,128)(2,1)} %bitcast.4, f32[3,1,1,4]{3,2,1,0:T(1,128)} %ext_in.1, bf16[512,512]{1,0:T(8,128)(2,1)} %constant.12.clone.first_in, bf16[2,256,256]{2,1,0:T(8,128)(2,1)} %constant.13.clone.near_in, bf16[1536,256]{1,0:T(8,128)(2,1)} %constant.14.clone.face_in, ...), custom_call_target="tpu_custom_call" | custom-call | flops 400000000 | bytes 3000000 | tf_op jit(solution)/shard_map/pipe/pallas_call | solution.py:607
  19.0 3.1 %basis.1 = (bf16[16,3,4,512]{3,2,1,0:T(4,128)(2,1)}, f32[16,16]{1,0:T(8,128)}, f32[16,15]{1,0:T(8,128)}) custom-call(f32[2,128]{1,0:T(2,128)} %get-tuple-element.8.total_ref, bf16[12,32,512]{2,1,0:T(8,128)(2,1)} %get-tuple-element.9.z_in), custom_call_target="tpu_custom_call" | custom-call | tf_op jit(solution)/shard_map/basis/pallas_call | solution.py:645

commit v7 on v6

--- a/solution.py
+++ b/solution.py
@@ -63,7 +63,12 @@
     node = np.arange(512)
     i2, i3 = (node // 8) % 8, node % 8
     picks = np.concatenate([node[i3 == 0], node[i3 == 7], node[i2 == 0], node[i2 == 7]])
-    faces = np.concatenate([table[:, picks] for table in full], axis=0)
+    faces = np.stack(
+        [
+            np.concatenate([table[:, picks[first : first + 128]] for table in full], axis=0)
+            for first in (0, 128)
+        ]
+    )
     spread = np.zeros((2, 128, 512), np.float32)
     for which in range(2):
         spread[which, np.arange(128), picks[128 * which : 128 * which + 128]] = 1.0
@@ -152,7 +157,8 @@
             [
                 (vel_in, vel_ref),
                 (ext_in, ext_ref),
-                (face_in, face_ref),
+                (face_in.at[0], face_ref.at[0]),
+                (face_in.at[1], face_ref.at[1]),
                 (first_in, first_ref),
                 (near_in, near_ref),
                 (spread_in, spread_ref),
@@ -223,17 +229,15 @@
                 out.append((lead * extent[c][e]) * one - (lead * extent[b][e]) * two)
         return out
 
-    loads[2].wait()
-    for load in loads[3:]:
-        load.start()
-    grads = [dot(pair[k], face_ref[pl.ds(k * nodes, nodes), :]) for k in range(3)]
-    raw = curl(grads)
     lane = lax.broadcasted_iota(jnp.int32, (snaps, 128), 1)
     place = lane % 64
     at_low, at_high = place < 8, place >= 56
-    faces = [[], []]
-    for which in range(2):
-        cut = [block[:, 128 * which : 128 * which + 128] for block in raw]
+    blank = jnp.zeros((snaps, 128), F32)
+
+    def make_faces(which):
+        grads = [dot(pair[k], face_ref[which, pl.ds(k * nodes, nodes), :]) for k in range(3)]
+        cut = curl(grads)
+        out = []
         for a in range(3):
             for e in range(radial):
                 value = cut[a * radial + e]
@@ -241,7 +245,10 @@
                     value += jnp.where(at_low, pltpu.roll(cut[a * radial + e - 1], 72, 1), 0.0)
                 if e < radial - 1:
                     value += jnp.where(at_high, pltpu.roll(cut[a * radial + e + 1], 56, 1), 0.0)
-                faces[which].append(value)
+                out.append(value)
+        out.append(mass)
+        return out + [blank] * (blocks - len(out))
+
     line = lax.broadcasted_iota(jnp.int32, (snaps, 128), 0)
     mass = jnp.zeros((snaps, 128), F32)
     for e in range(radial):
@@ -251,11 +258,10 @@
         if e < radial - 1:
             row += jnp.where(at_high, volume[e + 1], 0.0)
         mass = jnp.where(line == e, row, mass)
-    blank = jnp.zeros((snaps, 128), F32)
-    for which in range(2):
-        faces[which].append(mass)
-        while len(faces[which]) < blocks:
-            faces[which].append(blank)
+    loads[2].wait()
+    for load in loads[3:]:
+        load.start()
+    faces = {0: make_faces(0)}
     left = lane < 64
 
     def packed(which, p):
@@ -315,6 +321,8 @@
     ]
     for copy in wide_copies + edge_copies:
         copy.start()
+    loads[3].wait()
+    faces[1] = make_faces(1)
     for p in range(pairs):
         low, high = packed(1, p)
         send_narrow[0, p] = high
@@ -323,7 +331,7 @@
     for copy in narrow_copies:
         copy.start()
 
-    for load in loads[3:]:
+    for load in loads[4:]:
         load.wait()
     near = [near_ref[0], near_ref[1]]
     whole = [dot(pair[0], first_ref[...])]
@@ -526,7 +534,7 @@
 
 
 def basis_kernel(
-    row_count, radial, total_ref, z_in, q_ref, r_ref, dmd_ref, z_ref, rows_ref, z_sem
+    row_count, radial, total_ref, z_in, q_ref, r_ref, dmd_ref, z_ref, z_sem
 ):
     snaps, nodes = q_ref.shape[0], q_ref.shape[3]
     fields = 3 * radial
@@ -561,18 +569,29 @@
     inverse = pltpu.roll(work, 128 - snaps, 1)
     big, small = split(inverse * norm)
     weights = jnp.where(lane < 2 * snaps, big.astype(F32), small.astype(F32))
-    weights = weights[:, : 3 * snaps].astype(BF16)
+    weights = jnp.where(lane < 4 * snaps, weights, 0.0)
+    turned = pltpu.roll(weights, 4 * snaps, 1)
+    both = jnp.where(lane < 4 * snaps, weights, turned)
+    rows = []
+    for s in range(snaps):
+        rows.append(jnp.broadcast_to(both[s : s + 1, :], (radial, 128)))
+    rows = jnp.concatenate(rows, axis=0)
+    wide_line = lax.broadcasted_iota(jnp.int32, rows.shape, 0) % radial
+    wide_lane = lax.broadcasted_iota(jnp.int32, rows.shape, 1) // (4 * snaps)
+    per = 128 // (4 * snaps)
+    expanded = jnp.concatenate(
+        [
+            jnp.where(wide_line == wide_lane + per * i, rows, 0.0).astype(BF16)
+            for i in range(radial // per)
+        ],
+        axis=1,
+    )
     load.wait()
-    for b in range(fields):
-        basis = dot(weights, jnp.concatenate([z_ref[b], z_ref[b, 0:snaps, :]], axis=0))
-        for j in range(nodes // 128):
-            rows_ref[j, pl.ds(b, snaps, stride=fields), :] = basis[:, 128 * j : 128 * j + 128]
-    for s in range(snaps):
-        for c in range(3):
-            value = [
-                rows_ref[j, pl.ds((s * 3 + c) * radial, radial), :] for j in range(nodes // 128)
-            ]
-            q_ref[s, c] = jnp.concatenate(value, axis=1).astype(BF16)
+    for c in range(3):
+        held = [z_ref[c * radial + e] for e in range(radial)]
+        basis = dot(expanded, jnp.concatenate([h for h in held for _ in range(2)], axis=0))
+        for s in range(snaps):
+            q_ref[s, c] = basis[s * radial : (s + 1) * radial, :].astype(BF16)
     upper = jnp.where(jnp.logical_and(lane >= line, lane < snaps), work, 0.0)
     r_ref[...] = upper[:, :snaps] / norm
     moved = jnp.where(lane < snaps - 1, pltpu.roll(upper, 127, 1), 0.0)
@@ -614,7 +633,7 @@
             for i, operand in enumerate(operands)
         ]
         + [
-            dma((len(operands),)),
+            dma((len(operands) + 1,)),
             pltpu.VMEM((nodes // 128, fields * snaps, 128), F32),
             pltpu.VMEM((fields * snaps, nodes), BF16),
             pltpu.VMEM((fields, 2 * snaps, nodes), BF16),
@@ -653,7 +672,6 @@
         out_specs=(vmem, vmem, vmem),
         scratch_shapes=[
             pltpu.VMEM((fields, 2 * snaps, nodes), BF16),
-            pltpu.VMEM((nodes // 128, fields * snaps, 128), F32),
             dma(()),
         ],
         compiler_params=pltpu.CompilerParams(vmem_limit_bytes=limit),

time: 22.2 us -> 22.3 us (level)
  no operation moved by 1% of the time
where the time goes in v7:
time: 22.3 us; the launch traced here: 22.2 us
  Pallas kernels  21.5 us (96%)
  between operations  0.64 us (3%)
    pallas_call x1, Pallas kernels, shards(): pl.pallas_call(functools.partial(kernel, wide_count, narrow_count), out_s...  18.3 us
    pallas_call x1, Pallas kernels, shards(): pl.pallas_call(functools.partial(basis_kernel, row_count, radial), out_sh...  3.22 us

profile of v7, /device:TPU:0, one launch (start us, length us, event | category | flops | bytes accessed | tf_op | source)
XLA Modules:
  0.0 22.2 jit_solution(16431808349060721219)
XLA Ops:
  0.6 18.3 %pipe.1 = (bf16[12,32,512]{2,1,0:T(8,128)(2,1)}, f32[2,128]{1,0:T(2,128)}) custom-call(bf16[16,3,4,512]{3,2,1,0:T(4,128)(2,1)} %bitcast.4, f32[3,1,1,4]{3,2,1,0:T(1,128)} %ext_in.1, bf16[512,512]{1,0:T(8,128)(2,1)} %constant.12.clone.first_in, bf16[2,256,256]{2,1,0:T(8,128)(2,1)} %constant.13.clone.near_in, bf16[2,1536,128]{2,1,0:T(8,128)(2,1)} %constant.14.clone.face_in, ...), custom_call_target="tpu_custom_call" | custom-call | flops 400000000 | bytes 3000000 | tf_op jit(solution)/shard_map/pipe/pallas_call | solution.py:626
  19.0 3.2 %basis.1 = (bf16[16,3,4,512]{3,2,1,0:T(4,128)(2,1)}, f32[16,16]{1,0:T(8,128)}, f32[16,15]{1,0:T(8,128)}) custom-call(f32[2,128]{1,0:T(2,128)} %get-tuple-element.8.total_ref, bf16[12,32,512]{2,1,0:T(8,128)(2,1)} %get-tuple-element.9.z_in), custom_call_target="tpu_custom_call" | custom-call | tf_op jit(solution)/shard_map/basis/pallas_call | solution.py:664

commit v8 on v4

--- a/solution.py
+++ b/solution.py
@@ -519,11 +519,12 @@
     work = jnp.where(lane < snaps, work, jnp.where(unit, 1.0, 0.0))
     for k in range(0, snaps - 1, 2):
         row_a, row_b = work[k : k + 1, :], work[k + 1 : k + 2, :]
-        col_a, col_b = work[:, k : k + 1], work[:, k + 1 : k + 2]
-        inv_a = 1.0 / work[k : k + 1, k : k + 1]
-        cross = work[k : k + 1, k + 1 : k + 2]
+        col_a = jnp.broadcast_to(work[:, k : k + 1], work.shape)
+        col_b = jnp.broadcast_to(work[:, k + 1 : k + 2], work.shape)
+        inv_a = 1.0 / col_a[k : k + 1, :]
+        cross = col_b[k : k + 1, :]
         ratio = cross * inv_a
-        inv_b = 1.0 / (work[k + 1 : k + 2, k + 1 : k + 2] - cross * ratio)
+        inv_b = 1.0 / (col_b[k + 1 : k + 2, :] - cross * ratio)
         row_b = row_b - ratio * row_a
         col_b = col_b - ratio * col_a
         after = work - col_a * (inv_a * row_a) - col_b * (inv_b * row_b)

time: 22 us -> 21.5 us (0.977)
  Pallas kernels: 21.2 us -> 20.7 us
    pallas_call x1, Pallas kernels: 3.11 us -> 2.61 us  [shards(): pl.pallas_call(functools.partial(basis_kernel, row_count, radial), out_sh...]
where the time goes in v8:
time: 21.5 us; the launch traced here: 21.3 us
  Pallas kernels  20.7 us (96%)
  between operations  0.64 us (3%)
    pallas_call x1, Pallas kernels, shards(): pl.pallas_call(functools.partial(kernel, wide_count, narrow_count), out_s...  18.1 us
    pallas_call x1, Pallas kernels, shards(): pl.pallas_call(functools.partial(basis_kernel, row_count, radial), out_sh...  2.61 us

profile of v8, /device:TPU:0, one launch (start us, length us, event | category | flops | bytes accessed | tf_op | source)
XLA Modules:
  0.0 21.3 jit_solution(15068096240265707402)
XLA Ops:
  0.6 18.1 %pipe.1 = (bf16[32,6144]{1,0:T(8,128)(2,1)}, f32[2,128]{1,0:T(2,128)}) custom-call(bf16[16,3,4,512]{3,2,1,0:T(4,128)(2,1)} %bitcast.4, f32[3,1,1,4]{3,2,1,0:T(1,128)} %ext_in.1, bf16[512,512]{1,0:T(8,128)(2,1)} %constant.12.clone.first_in, bf16[2,256,256]{2,1,0:T(8,128)(2,1)} %constant.13.clone.near_in, bf16[1536,256]{1,0:T(8,128)(2,1)} %constant.14.clone.face_in, ...), custom_call_target="tpu_custom_call" | custom-call | flops 400000000 | bytes 3000000 | tf_op jit(solution)/shard_map/pipe/pallas_call | solution.py:582
  18.7 2.6 %basis.1 = (bf16[16,3,4,512]{3,2,1,0:T(4,128)(2,1)}, f32[16,16]{1,0:T(8,128)}, f32[16,15]{1,0:T(8,128)}) custom-call(f32[2,128]{1,0:T(2,128)} %get-tuple-element.8.total_ref, bf16[32,6144]{1,0:T(8,128)(2,1)} %get-tuple-element.9.z_in), custom_call_target="tpu_custom_call" | custom-call | tf_op jit(solution)/shard_map/basis/pallas_call | solution.py:621
